TPU v7x, 256 devices: a whole 4x4x8 slice. The times are simulated.
256 devices in a mesh: ctx: 32 (over z, y_hi, core), chan: 8 (over x, y_lo).
Axes of the slice: x: 4, y: 4 (y_hi: 2, y_lo: 2; y = y_hi * 2 + y_lo), z: 8, core: 2. Of those that a mesh axis runs over, the one named last changes fastest.
Arguments:
- query_gate: bfloat16 [16384, 4096], P('ctx', 'chan'), may hold values from -600 to 600
- key_branch: bfloat16 [16384, 4096], P('ctx', 'chan'), may hold values from -6 to 6
- value_branch: bfloat16 [16384, 4096], P('ctx', 'chan'), may hold values from -6 to 6
- conv_filter: float32 [16384, 4096], P('ctx', 'chan'), may hold values from -1.1 to 1.1
- skip_weight: float32 [4096], P('chan'), may hold values from 0.5 to 1.5
- norm_gain: float32 [4096], P('chan'), may hold values from 0.25 to 1.75
Outputs:
- layer_out: bfloat16 [16384, 4096], P('ctx', 'chan')
All inputs are finite; a program needn't handle non-finite values.
Results may differ from a plain program's by a relative error of at most 0.0022.
Values sent between devices are 32-bit elements; how exact they have to be, the bound alone decides.
No kernel may reach another device: no remote copies, remote signals or barrier semaphores. Data moves between devices by JAX's collectives and lax.ppermute only.
A program may use at most 128 MiB of HBM per device.

v0:
```python
import math

import jax
import jax.numpy as jnp
from jax import lax
from jax.sharding import PartitionSpec as P

CH = 4096


HIGHEST = lax.Precision.HIGHEST


def angles(row_index, col_index, period):
    phases = row_index[:, None] * col_index[None, :] % period
    return phases.astype(jnp.float32) * (2.0 * math.pi / period)


def apply_rows(matrix, values):
    return jnp.einsum(
        "ab,bsc->asc", matrix, values, precision=HIGHEST, preferred_element_type=jnp.float32
    )


def along_second(matrix, values):
    return jnp.einsum(
        "kn,anc->akc", matrix, values, precision=HIGHEST, preferred_element_type=jnp.float32
    )


def rotate(real_part, imag_part, cosine, sine_part):
    return (real_part * cosine - imag_part * sine_part, real_part * sine_part + imag_part * cosine)


def on_device(query_gate, key_branch, value_branch, conv_filter, skip_weight, norm_gain):
    blocks = lax.axis_size("ctx")
    my_block = lax.axis_index("ctx")
    tokens = key_branch.shape[0]
    stride = tokens // blocks
    period = 2 * blocks * tokens
    product = key_branch.astype(jnp.float32) * value_branch.astype(jnp.float32)
    low_freq = jnp.arange(blocks, dtype=jnp.int32)
    high_freq = jnp.where(low_freq == 0, blocks, 2 * blocks - low_freq)
    freq_order = jnp.stack([low_freq, high_freq], axis=1).reshape(2 * blocks)
    outer_angle = angles(freq_order, low_freq, 2 * blocks)
    outer_cos, outer_sin = (jnp.cos(outer_angle), jnp.sin(outer_angle))
    local_pos = my_block * stride + jnp.arange(stride, dtype=jnp.int32)
    twiddle = angles(freq_order, local_pos, period)
    twiddle_cos, twiddle_sin = (jnp.cos(twiddle)[:, :, None], jnp.sin(twiddle)[:, :, None])
    all_pos = jnp.arange(tokens, dtype=jnp.int32)
    inner_angle = angles(all_pos, all_pos, tokens)
    inner_cos, inner_sin = (jnp.cos(inner_angle), jnp.sin(inner_angle))
    held_freq = lax.dynamic_slice_in_dim(freq_order, 2 * my_block, 2)
    back_angle = angles(held_freq, all_pos, period)
    back_cos, back_sin = (jnp.cos(back_angle)[:, :, None], jnp.sin(back_angle)[:, :, None])

    def forward(real_part, imag_part):
        spec_re = along_second(inner_cos, real_part) + along_second(inner_sin, imag_part)
        spec_im = along_second(inner_cos, imag_part) - along_second(inner_sin, real_part)
        return (spec_re, spec_im)

    signal = lax.all_to_all(product[None], "ctx", split_axis=1, concat_axis=0, tiled=True)
    kernel = lax.all_to_all(conv_filter[None], "ctx", split_axis=1, concat_axis=0, tiled=True)
    cos_signal = apply_rows(outer_cos, signal)
    sin_signal = apply_rows(outer_sin, signal)
    cos_kernel = apply_rows(outer_cos, kernel)
    sin_kernel = apply_rows(outer_sin, kernel)
    signal_re, signal_im = rotate(cos_signal, -sin_signal, twiddle_cos, -twiddle_sin)
    kernel_re, kernel_im = rotate(cos_kernel, -sin_kernel, twiddle_cos, -twiddle_sin)
    apart_signal_re, apart_signal_im = forward(
        lax.all_to_all(signal_re, "ctx", split_axis=0, concat_axis=1, tiled=True),
        lax.all_to_all(signal_im, "ctx", split_axis=0, concat_axis=1, tiled=True),
    )
    apart_kernel_re, apart_kernel_im = forward(
        lax.all_to_all(kernel_re, "ctx", split_axis=0, concat_axis=1, tiled=True),
        lax.all_to_all(kernel_im, "ctx", split_axis=0, concat_axis=1, tiled=True),
    )
    spec_re = apart_signal_re * apart_kernel_re - apart_signal_im * apart_kernel_im
    spec_im = apart_signal_re * apart_kernel_im + apart_signal_im * apart_kernel_re
    time_re = along_second(inner_cos, spec_re) - along_second(inner_sin, spec_im)
    time_im = along_second(inner_cos, spec_im) + along_second(inner_sin, spec_re)
    turned_re, turned_im = rotate(time_re, time_im, back_cos, back_sin)
    time_re = lax.all_to_all(turned_re, "ctx", split_axis=1, concat_axis=0, tiled=True)
    time_im = lax.all_to_all(turned_im, "ctx", split_axis=1, concat_axis=0, tiled=True)
    last_angle = angles(low_freq, freq_order, 2 * blocks)
    last_cos, last_sin = (jnp.cos(last_angle), jnp.sin(last_angle))
    conv_part = (apply_rows(last_cos, time_re) - apply_rows(last_sin, time_im)) / period
    convolved = lax.all_to_all(conv_part, "ctx", split_axis=0, concat_axis=1, tiled=True)[0]
    gated = query_gate.astype(jnp.float32) * (convolved + skip_weight[None, :] * product)
    partial_value = jnp.sum(gated * gated, axis=1)
    total_sq = lax.psum(partial_value, "chan")
    inverse_rms = lax.rsqrt(total_sq / CH + 1e-05)
    return (gated * inverse_rms[:, None] * norm_gain[None, :]).astype(jnp.bfloat16)


def solution(mesh):
    in_specs = (
        P("ctx", "chan"),
        P("ctx", "chan"),
        P("ctx", "chan"),
        P("ctx", "chan"),
        P("chan"),
        P("chan"),
    )
    out_specs = P("ctx", "chan")
    return jax.shard_map(
        on_device, mesh=mesh, in_specs=in_specs, out_specs=out_specs, check_vma=False
    )
```

profile of v0, /device:TPU:16, one launch (start us, length us, event | category | flops | bytes accessed | tf_op | source)
XLA Modules:
  0.0 585.4 jit_solution(8492496864412369310)
XLA Ops:
  3.5 11.6 %all-to-all-start = ((f32[1,512,512]{2,0,1:T(1,128)}), f32[1,512,512]{2,0,1:T(1,128)S(1)}, u32[]{:S(2)}, u32[]{:S(2)}) async-start(f32[1,512,512]{2,0,1:T(1,128)} %copy.60), calls=%async_computation | async-start | bytes 2097152 | tf_op jit(solution)/shard_map/all_to_all | solution.py:62
  16.8 27.2 %all-to-all-done = f32[1,512,512]{2,0,1:T(1,128)S(1)} async-done(((f32[1,512,512]{2,0,1:T(1,128)}), f32[1,512,512]{2,0,1:T(1,128)S(1)}, u32[]{:S(2)}, u32[]{:S(2)}) %all-to-all-start) | async-done | bytes 1048608 | tf_op jit(solution)/shard_map/all_to_all | solution.py:62
  57.2 20.9 %all-to-all-done.3 = f32[1,512,512]{2,0,1:T(1,128)S(1)} async-done(((f32[1,512,512]{2,0,1:T(1,128)}), f32[1,512,512]{2,0,1:T(1,128)S(1)}, u32[]{:S(2)}, u32[]{:S(2)}) %all-to-all-start.3) | async-done | bytes 1048608 | tf_op jit(solution)/shard_map/all_to_all | solution.py:63
  97.1 46.1 %all-to-all-done.5 = f32[64,16,512]{2,1,0:T(8,128)} async-done(((f32[64,16,512]{2,1,0:T(8,128)}), f32[64,16,512]{2,1,0:T(8,128)}, u32[]{:S(2)}, u32[]{:S(2)}) %all-to-all-start.5) | async-done | bytes 2097184 | tf_op jit(solution)/shard_map/all_to_all | solution.py:76
  154.0 46.2 %all-to-all-done.4 = f32[64,16,512]{2,1,0:T(8,128)} async-done(((f32[64,16,512]{2,1,0:T(8,128)}), f32[64,16,512]{2,1,0:T(8,128)}, u32[]{:S(2)}, u32[]{:S(2)}) %all-to-all-start.4) | async-done | bytes 2097184 | tf_op jit(solution)/shard_map/all_to_all | solution.py:75
  209.0 47.7 %all-to-all-done.2 = f32[64,16,512]{2,1,0:T(8,128)} async-done(((f32[64,16,512]{2,1,0:T(8,128)}), f32[64,16,512]{2,1,0:T(8,128)}, u32[]{:S(2)}, u32[]{:S(2)}) %all-to-all-start.2) | async-done | bytes 2097184 | tf_op jit(solution)/shard_map/all_to_all | solution.py:72
  268.7 10.9 %fusion.27 = f32[2,512,512]{2,1,0:T(8,128)S(1)} fusion(f32[2,512,512]{2,1,0:T(8,128)S(1)} %bitcast.122), kind=kOutput, calls=%fused_computation.40 | convolution fusion | flops 3224895488 | bytes 4194304 | tf_op jit(solution)/shard_map/kn,anc->akc/dot_general | solution.py:26
  279.7 10.9 %fusion.31 = f32[2,512,512]{2,1,0:T(8,128)S(1)} fusion(f32[2,512,512]{2,1,0:T(8,128)S(1)} %bitcast.126), kind=kOutput, calls=%fused_computation.44 | convolution fusion | flops 3224895488 | bytes 4194304 | tf_op jit(solution)/shard_map/kn,anc->akc/dot_general | solution.py:26
  290.6 11.8 %fusion.29 = f32[2,512,512]{2,1,0:T(8,128)} fusion(f32[2,512,512]{2,1,0:T(8,128)S(1)} %bitcast.120), kind=kOutput, calls=%fused_computation.42 | convolution fusion | flops 3224895488 | bytes 4194304 | tf_op jit(solution)/shard_map/kn,anc->akc/dot_general | solution.py:26
  302.3 11.2 %convolution_subtract_fusion = f32[2,512,512]{2,1,0:T(8,128)S(1)} fusion(f32[2,512,512]{2,1,0:T(8,128)S(1)} %fusion.27, f32[2,512,512]{2,1,0:T(8,128)S(1)} %bitcast.127), kind=kOutput, calls=%fused_computation.18 | convolution fusion | flops 3225419776 | bytes 6291456 | tf_op jit(solution)/shard_map/kn,anc->akc/dot_general | solution.py:26
  313.6 11.8 %convolution_add_fusion = f32[2,512,512]{2,1,0:T(8,128)} fusion(f32[2,512,512]{2,1,0:T(8,128)S(1)} %fusion.31, f32[2,512,512]{2,1,0:T(8,128)S(1)} %bitcast.123), kind=kOutput, calls=%fused_computation.20 | convolution fusion | flops 3225419776 | bytes 6291456 | tf_op jit(solution)/shard_map/kn,anc->akc/dot_general | solution.py:26
  327.2 10.9 %fusion.33 = f32[2,512,512]{2,1,0:T(8,128)S(1)} fusion(f32[2,512,512]{2,1,0:T(8,128)S(1)} %bitcast.124), kind=kOutput, calls=%fused_computation.46 | convolution fusion | flops 3224895488 | bytes 4194304 | tf_op jit(solution)/shard_map/kn,anc->akc/dot_general | solution.py:26
  338.1 11.6 %convolution_add_fusion.1 = f32[2,512,512]{2,1,0:T(8,128)S(1)} fusion(f32[2,512,512]{2,1,0:T(8,128)S(1)} %fusion.33, f32[2,512,512]{2,1,0:T(8,128)S(1)} %bitcast.121), kind=kOutput, calls=%fused_computation.21 | convolution fusion | flops 3225419776 | bytes 6291456 | tf_op jit(solution)/shard_map/kn,anc->akc/dot_general | solution.py:26
  349.7 11.6 %multiply_subtract_fusion = (f32[2,512,512]{2,1,0:T(8,128)S(1)}, f32[2,512,512]{2,1,0:T(8,128)S(1)}) fusion(f32[2,512,512]{2,1,0:T(8,128)S(1)} %convolution_subtract_fusion, f32[2,512,512]{2,1,0:T(8,128)S(1)} %convolution_add_fusion.1, f32[2,512,512]{2,1,0:T(8,128)S(1)} %copy-done, f32[2,512,512]{2,1,0:T(8,128)S(1)} %copy-done.7, ...), kind=kOutput, calls=%fused_computation.11 | convolution fusion | flops 3228565504 | bytes 14680064 | tf_op jit(solution)/shard_map/kn,anc->akc/dot_general | solution.py:26
  361.4 8.6 %fusion = f32[2,512,512]{2,1,0:T(8,128)S(1)} fusion(f32[2,512,512]{2,1,0:T(8,128)S(1)} %get-tuple-element.6), kind=kOutput, calls=%fused_computation | convolution fusion | flops 3224895488 | bytes 4194304 | tf_op jit(solution)/shard_map/kn,anc->akc/dot_general | solution.py:26
  369.9 8.4 %fusion.2 = f32[2,512,512]{2,1,0:T(8,128)S(1)} fusion(f32[2,512,512]{2,1,0:T(8,128)S(1)} %get-tuple-element.6), kind=kOutput, calls=%fused_computation.2 | convolution fusion | flops 3224895488 | bytes 4194304 | tf_op jit(solution)/shard_map/kn,anc->akc/dot_general | solution.py:26
  378.4 8.7 %fusion.8 = f32[2,512,512]{2,1,0:T(8,128)S(1)} fusion(f32[2,512,512]{2,1,0:T(8,128)S(1)} %fusion.2, f32[2,512,512]{2,1,0:T(8,128)S(1)} %get-tuple-element.5), kind=kOutput, calls=%fused_computation.16 | convolution fusion | flops 3225419776 | bytes 6291456 | tf_op jit(solution)/shard_map/kn,anc->akc/dot_general | solution.py:26
  387.0 9.7 %add_bitcast_fusion = (f32[2,512,512]{1,2,0:T(8,128)S(1)}, f32[2,512,512]{1,2,0:T(8,128)}) fusion(f32[2,512,512]{2,1,0:T(8,128)S(1)} %fusion.8, f32[2,512]{1,0:T(2,128)S(1)} %get-tuple-element.18, f32[2,512]{1,0:T(2,128)S(1)} %get-tuple-element.17, f32[2,512,512]{2,1,0:T(8,128)S(1)} %fusion, f32[2,512,512]{2,1,0:T(8,128)S(1)} %get-tuple-element.5), kind=kOutput, calls=%fused_computation.8 | convolution fusion | flops 3228565504 | bytes 10493952 | tf_op jit(solution)/shard_map/kn,anc->akc/dot_general | solution.py:26
  399.2 9.8 %all-to-all-start.7 = ((f32[2,512,512]{2,0,1:T(2,128)}), f32[2,512,512]{2,0,1:T(2,128)S(1)}, u32[]{:S(2)}, u32[]{:S(2)}) async-start(f32[2,512,512]{2,0,1:T(2,128)} %copy.84), calls=%async_computation.7 | async-start | bytes 4194304 | tf_op jit(solution)/shard_map/all_to_all | solution.py:84
  413.1 46.1 %all-to-all-done.7 = f32[2,512,512]{2,0,1:T(2,128)S(1)} async-done(((f32[2,512,512]{2,0,1:T(2,128)}), f32[2,512,512]{2,0,1:T(2,128)S(1)}, u32[]{:S(2)}, u32[]{:S(2)}) %all-to-all-start.7) | async-done | bytes 2097184 | tf_op jit(solution)/shard_map/all_to_all | solution.py:84
  459.2 6.7 %all-to-all-start.6 = ((f32[2,512,512]{2,0,1:T(2,128)}), f32[2,512,512]{2,0,1:T(2,128)}, u32[]{:S(2)}, u32[]{:S(2)}) async-start(f32[2,512,512]{2,0,1:T(2,128)} %copy.81), calls=%async_computation.6 | async-start | bytes 4194304 | tf_op jit(solution)/shard_map/all_to_all | solution.py:83
  472.0 44.0 %all-to-all-done.6 = f32[2,512,512]{2,0,1:T(2,128)} async-done(((f32[2,512,512]{2,0,1:T(2,128)}), f32[2,512,512]{2,0,1:T(2,128)}, u32[]{:S(2)}, u32[]{:S(2)}) %all-to-all-start.6) | async-done | bytes 2097184 | tf_op jit(solution)/shard_map/all_to_all | solution.py:83
  529.2 34.9 %all_to_all.141 = f32[32,16,512]{2,1,0:T(8,128)S(1)} all-to-all(f32[32,16,512]{2,1,0:T(8,128)S(1)} %copy.87), channel_id=1, replica_groups=mesh['ctx'=32,'chan'=8] {'ctx'}, dimensions={0} | all-to-all | bytes 2097152 | tf_op jit(solution)/shard_map/all_to_all | solution.py:88
  564.5 19.4 %psum.7 = f32[512]{0:T(512)S(1)} all-reduce(f32[512]{0:T(512)S(1)} %multiply_reduce_fusion), channel_id=1, replica_groups=mesh['ctx'=32,'chan'=8] {'chan'}, use_global_device_ids=true, to_apply=%region_1.2 | all-reduce | flops 512 | bytes 4096 | tf_op jit(solution)/shard_map/psum | solution.py:91
  (70 shorter events, 98.0 us)
Async XLA Ops:
  1.4 13.7 %copy-start.9 = (f32[512,512]{1,0:T(8,128)S(1)}, f32[512,512]{1,0:T(8,128)}, u32[]{:S(2)}) copy-start(f32[512,512]{1,0:T(8,128)} %param.9) | copy-start | bytes 3145732
  3.5 40.5 %all-to-all-start = ((f32[1,512,512]{2,0,1:T(1,128)}), f32[1,512,512]{2,0,1:T(1,128)S(1)}, u32[]{:S(2)}, u32[]{:S(2)}) async-start(f32[1,512,512]{2,0,1:T(1,128)} %copy.60), calls=%async_computation | async-start | bytes 2097152 | tf_op jit(solution)/shard_map/all_to_all | solution.py:62
  44.0 34.1 %all-to-all-start.3 = ((f32[1,512,512]{2,0,1:T(1,128)}), f32[1,512,512]{2,0,1:T(1,128)S(1)}, u32[]{:S(2)}, u32[]{:S(2)}) async-start(f32[1,512,512]{2,0,1:T(1,128)} %broadcast_in_dim.10), calls=%async_computation.3 | async-start | bytes 2097152 | tf_op jit(solution)/shard_map/all_to_all | solution.py:63
  78.1 2.5 copy-start.4
  78.2 2.4 copy-start.3
  87.9 55.4 %all-to-all-start.5 = ((f32[64,16,512]{2,1,0:T(8,128)}), f32[64,16,512]{2,1,0:T(8,128)}, u32[]{:S(2)}, u32[]{:S(2)}) async-start(f32[64,16,512]{2,1,0:T(8,128)} %copy.74), calls=%async_computation.5 | async-start | bytes 4194304 | tf_op jit(solution)/shard_map/all_to_all | solution.py:76
  143.2 56.9 %all-to-all-start.4 = ((f32[64,16,512]{2,1,0:T(8,128)}), f32[64,16,512]{2,1,0:T(8,128)}, u32[]{:S(2)}, u32[]{:S(2)}) async-start(f32[64,16,512]{2,1,0:T(8,128)} %copy.71), calls=%async_computation.4 | async-start | bytes 4194304 | tf_op jit(solution)/shard_map/all_to_all | solution.py:75
  200.2 56.5 %all-to-all-start.2 = ((f32[64,16,512]{2,1,0:T(8,128)}), f32[64,16,512]{2,1,0:T(8,128)}, u32[]{:S(2)}, u32[]{:S(2)}) async-start(f32[64,16,512]{2,1,0:T(8,128)} %copy.66), calls=%async_computation.2 | async-start | bytes 4194304 | tf_op jit(solution)/shard_map/all_to_all | solution.py:72
  256.7 68.7 %all-to-all-start.1 = ((f32[64,16,512]{2,1,0:T(8,128)}), f32[64,16,512]{2,1,0:T(8,128)}, u32[]{:S(2)}, u32[]{:S(2)}) async-start(f32[64,16,512]{2,1,0:T(8,128)} %copy.63), calls=%async_computation.1 | async-start | bytes 4194304 | tf_op jit(solution)/shard_map/all_to_all | solution.py:71
  268.7 21.9 %copy-start.1 = (f32[2,32,16,512]{3,2,1,0:T(8,128)}, f32[2,32,16,512]{3,2,1,0:T(8,128)S(1)}, u32[]{:S(2)}) copy-start(f32[2,32,16,512]{3,2,1,0:T(8,128)S(1)} %copy.67) | copy-start | bytes 6291460
  327.2 10.9 %copy-start.2 = (f32[2,32,16,512]{3,2,1,0:T(8,128)S(1)}, f32[2,32,16,512]{3,2,1,0:T(8,128)}, u32[]{:S(2)}) copy-start(f32[2,32,16,512]{3,2,1,0:T(8,128)} %copy-done.1) | copy-start | bytes 6291460
  338.0 11.7 %copy-start = (f32[2,512,512]{2,1,0:T(8,128)S(1)}, f32[2,512,512]{2,1,0:T(8,128)}, u32[]{:S(2)}) copy-start(f32[2,512,512]{2,1,0:T(8,128)} %convolution_add_fusion) | copy-start | bytes 6291460
  338.1 11.7 %copy-start.7 = (f32[2,512,512]{2,1,0:T(8,128)S(1)}, f32[2,512,512]{2,1,0:T(8,128)}, u32[]{:S(2)}) copy-start(f32[2,512,512]{2,1,0:T(8,128)} %fusion.29) | copy-start | bytes 6291460
  399.2 60.0 %all-to-all-start.7 = ((f32[2,512,512]{2,0,1:T(2,128)}), f32[2,512,512]{2,0,1:T(2,128)S(1)}, u32[]{:S(2)}, u32[]{:S(2)}) async-start(f32[2,512,512]{2,0,1:T(2,128)} %copy.84), calls=%async_computation.7 | async-start | bytes 4194304 | tf_op jit(solution)/shard_map/all_to_all | solution.py:84
  459.2 56.8 %all-to-all-start.6 = ((f32[2,512,512]{2,0,1:T(2,128)}), f32[2,512,512]{2,0,1:T(2,128)}, u32[]{:S(2)}, u32[]{:S(2)}) async-start(f32[2,512,512]{2,0,1:T(2,128)} %copy.81), calls=%async_computation.6 | async-start | bytes 4194304 | tf_op jit(solution)/shard_map/all_to_all | solution.py:83
  528.5 35.6 %copy-start.5 = (bf16[512,512]{1,0:T(8,128)(2,1)S(1)}, bf16[512,512]{1,0:T(8,128)(2,1)}, u32[]{:S(2)}) copy-start(bf16[512,512]{1,0:T(8,128)(2,1)} %param.8) | copy-start | bytes 1572868
  528.6 35.6 %copy-start.6 = (bf16[512,512]{1,0:T(8,128)(2,1)S(1)}, bf16[512,512]{1,0:T(8,128)(2,1)}, u32[]{:S(2)}) copy-start(bf16[512,512]{1,0:T(8,128)(2,1)} %param.7) | copy-start | bytes 1572868
  528.6 35.6 %copy-start.8 = (bf16[512,512]{1,0:T(8,128)(2,1)S(1)}, bf16[512,512]{1,0:T(8,128)(2,1)}, u32[]{:S(2)}) copy-start(bf16[512,512]{1,0:T(8,128)(2,1)} %param.6) | copy-start | bytes 1572868
  528.6 35.6 %copy-start.10 = (f32[512]{0:T(512)S(1)}, f32[512]{0:T(512)}, u32[]{:S(2)}) copy-start(f32[512]{0:T(512)} %param.10) | copy-start | bytes 6148
  529.2 54.8 %copy-start.11 = (f32[512]{0:T(512)S(1)}, f32[512]{0:T(512)}, u32[]{:S(2)}) copy-start(f32[512]{0:T(512)} %param.11) | copy-start | bytes 6148
where the time goes:
time: 589 us; the launch traced here: 585 us
  waiting for transfers between devices  278 us (47%)
  matrix products  145 us (25%)
  starting transfers between devices  57.4 us (10%)
  blocking collectives  54.3 us (9%)
  local copies, waits for them, and re-layouts  46.9 us (8%)
    dot_general x12, matrix products, along_second(): jnp.einsum('kn,anc->akc', matrix, values, precision=HIGHEST, preferred_el...  126 us
    all_to_all x1, waiting for transfers between devices, on_device(): lax.all_to_all(signal_im, 'ctx', split_axis=0, concat_axis=1, tiled=True)  47.7 us
    all_to_all x1, waiting for transfers between devices, on_device(): lax.all_to_all(kernel_re, 'ctx', split_axis=0, concat_axis=1, tiled=True)  46.2 us
    all_to_all x1, waiting for transfers between devices, on_device(): lax.all_to_all(turned_im, 'ctx', split_axis=1, concat_axis=0, tiled=True)  46.1 us
    all_to_all x1, waiting for transfers between devices, on_device(): lax.all_to_all(kernel_im, 'ctx', split_axis=0, concat_axis=1, tiled=True)  46.1 us
    all_to_all x1, waiting for transfers between devices, on_device(): lax.all_to_all(turned_re, 'ctx', split_axis=1, concat_axis=0, tiled=True)  44 us
    all_to_all x1, blocking collectives, on_device(): lax.all_to_all(conv_part, 'ctx', split_axis=0, concat_axis=1, tiled=True)[0]  34.9 us
    all_to_all x1, waiting for transfers between devices, on_device(): lax.all_to_all(product[None], 'ctx', split_axis=1, concat_axis=0, tiled=T...  27.2 us
  transfers between devices with their start and end apart: 8, of which 7 were waited for; matrix products, arithmetic and copies ran while one was open for 15% of the time, Pallas kernels for 0%

commit v1 on v0

v1 whole, which is shorter than its diff:
```python
import functools
import math

import jax
import jax.numpy as jnp
import ml_dtypes
import numpy as np
from jax import lax
from jax.experimental import pallas as pl
from jax.experimental.pallas import tpu as pltpu
from jax.sharding import PartitionSpec as P

CH = 4096
LANES = 128
F32 = jnp.float32
BF16 = jnp.bfloat16
VMEM_BYTES = 32 * 1024 * 1024


def split_const(values):
    high = values.astype(ml_dtypes.bfloat16)
    low = (values - high.astype(np.float64)).astype(ml_dtypes.bfloat16)
    return high, low


def transform_tables(rows, cols):
    length = rows * cols
    m = np.arange(rows, dtype=np.float64)
    b = np.arange(cols, dtype=np.float64)
    first = 2.0 * math.pi * np.outer(m + 0.25, m) / rows
    first_high, first_low = split_const(np.concatenate([np.cos(first), -np.sin(first)], axis=0))
    first_table = np.concatenate([first_high, first_high, first_low], axis=1)
    turn = 2.0 * math.pi * np.outer(m + 0.25, b) / length
    turn_re = np.cos(turn).astype(np.float32)
    turn_im = (-np.sin(turn)).astype(np.float32)
    second = 2.0 * math.pi * (np.outer(b, b) % cols) / cols
    cosine, sine = np.cos(second), np.sin(second)
    fwd_high, fwd_low = split_const(np.block([[cosine, -sine], [sine, cosine]]))
    fwd_table = np.concatenate([fwd_high, fwd_high, fwd_low], axis=0)
    back_high, back_low = split_const(np.block([[cosine, sine], [-sine, cosine]]))
    back_table = np.concatenate([back_high, back_high, back_low], axis=0)
    last_high, last_low = split_const(
        np.concatenate([np.cos(first.T), -np.sin(first.T)], axis=1) / length
    )
    last_table = np.concatenate([last_high, last_high, last_low], axis=1)
    return first_table, turn_re, turn_im, fwd_table, back_table, last_table


def split(values):
    high = values.astype(BF16)
    low = (values - high.astype(F32)).astype(BF16)
    return high, low


def dot(left, right):
    return jnp.dot(left, right, preferred_element_type=F32)


def pack_kernel(key_ref, value_ref, filter_ref, out_ref):
    share = out_ref.shape[3]
    product = key_ref[...].astype(F32) * value_ref[...].astype(F32)
    out_ref[:, 0, 0] = product.T.reshape(-1, share, LANES)
    out_ref[:, 0, 1] = filter_ref[...].T.reshape(-1, share, LANES)


def conv_kernel(
    group, share, data_ref, first_ref, turn_re_ref, turn_im_ref, fwd_ref, back_ref, last_ref, out_ref
):
    rows = turn_re_ref.shape[0]
    turn_re = jnp.concatenate([turn_re_ref[...]] * 2, axis=1)
    turn_im = jnp.concatenate([turn_im_ref[...]] * 2, axis=1)
    for start in range(0, share, group):
        parts = []
        for c in range(start, start + group):
            signal = data_ref[pl.ds(c, rows, stride=2 * share), :]
            kernel = data_ref[pl.ds(share + c, rows, stride=2 * share), :]
            high, low = split(jnp.concatenate([signal, kernel], axis=1))
            spec = dot(first_ref[...], jnp.concatenate([high, low, high], axis=0))
            re, im = spec[:rows], spec[rows:]
            out_re = re * turn_re - im * turn_im
            out_im = re * turn_im + im * turn_re
            parts.append(jnp.concatenate([out_re[:, :LANES], out_im[:, :LANES]], axis=1))
            parts.append(jnp.concatenate([out_re[:, LANES:], out_im[:, LANES:]], axis=1))
        high, low = split(jnp.concatenate(parts, axis=0))
        spec = dot(jnp.concatenate([high, low, high], axis=1), fwd_ref[...])
        parts = []
        for c in range(group):
            signal = spec[2 * c * rows : (2 * c + 1) * rows]
            kernel = spec[(2 * c + 1) * rows : (2 * c + 2) * rows]
            s_re, s_im = signal[:, :LANES], signal[:, LANES:]
            k_re, k_im = kernel[:, :LANES], kernel[:, LANES:]
            parts.append(
                jnp.concatenate([s_re * k_re - s_im * k_im, s_re * k_im + s_im * k_re], axis=1)
            )
        high, low = split(jnp.concatenate(parts, axis=0))
        spec = dot(jnp.concatenate([high, low, high], axis=1), back_ref[...])
        for c in range(0, group, 2):
            first = spec[c * rows : (c + 1) * rows]
            second = spec[(c + 1) * rows : (c + 2) * rows]
            re = jnp.concatenate([first[:, :LANES], second[:, :LANES]], axis=1)
            im = jnp.concatenate([first[:, LANES:], second[:, LANES:]], axis=1)
            turned = jnp.concatenate(
                [re * turn_re + im * turn_im, im * turn_re - re * turn_im], axis=0
            )
            high, low = split(turned)
            conv = dot(last_ref[...], jnp.concatenate([high, low, high], axis=0))
            out_ref[pl.ds(start + c, rows, stride=share), :] = conv[:, :LANES]
            out_ref[pl.ds(start + c + 1, rows, stride=share), :] = conv[:, LANES:]


def gate_kernel(conv_ref, query_ref, key_ref, value_ref, skip_ref, gated_ref, square_ref):
    conv = conv_ref[...].reshape(-1, LANES).T
    product = key_ref[...].astype(F32) * value_ref[...].astype(F32)
    gated = query_ref[...].astype(F32) * (conv + skip_ref[...] * product)
    gated_ref[...] = gated
    square = gated * gated
    folded = square[:, :LANES]
    for start in range(LANES, square.shape[1], LANES):
        folded = folded + square[:, start : start + LANES]
    total = jnp.sum(folded.T, axis=0, keepdims=True)
    square_ref[...] = jnp.broadcast_to(total, square_ref.shape)


def norm_kernel(gated_ref, square_ref, gain_ref, out_ref):
    total = jnp.sum(square_ref[...], axis=0, keepdims=True)
    inverse = lax.rsqrt(total / CH + 1e-05)
    spread = jnp.broadcast_to(inverse, (LANES, LANES)).T
    for start in range(0, out_ref.shape[1], LANES):
        at = slice(start, start + LANES)
        out_ref[:, at] = (gated_ref[:, at] * spread * gain_ref[:, at]).astype(BF16)


def on_device(query_gate, key_branch, value_branch, conv_filter, skip_weight, norm_gain):
    blocks = lax.axis_size("ctx")
    peers = lax.axis_size("chan")
    tokens, channels = key_branch.shape
    share = channels // blocks
    pieces = tokens // LANES
    rows = blocks * pieces
    params = pltpu.CompilerParams(vmem_limit_bytes=VMEM_BYTES)
    strip = pl.BlockSpec((LANES, channels), lambda a: (a, 0))
    row = pl.BlockSpec((1, channels), lambda a: (0, 0))
    packed = pl.pallas_call(
        pack_kernel,
        grid=(pieces,),
        in_specs=[strip] * 3,
        out_specs=pl.BlockSpec((blocks, 1, 2, share, LANES), lambda a: (0, a, 0, 0, 0)),
        out_shape=jax.ShapeDtypeStruct((blocks, pieces, 2, share, LANES), F32),
        compiler_params=params,
        name="pack",
    )(key_branch, value_branch, conv_filter)
    packed = packed.reshape(blocks, pieces * 2 * share, LANES)
    gathered = lax.all_to_all(packed, "ctx", split_axis=0, concat_axis=0, tiled=True)
    gathered = gathered.reshape(rows * 2 * share, LANES)
    tables = transform_tables(rows, LANES)
    conv = pl.pallas_call(
        functools.partial(conv_kernel, 4, share),
        out_shape=jax.ShapeDtypeStruct((rows * share, LANES), F32),
        compiler_params=params,
        name="conv",
    )(gathered, *tables)
    conv = conv.reshape(blocks, pieces * share, LANES)
    conv = lax.all_to_all(conv, "ctx", split_axis=0, concat_axis=0, tiled=True)
    conv = conv.reshape(blocks, pieces, share, LANES)
    gated, square = pl.pallas_call(
        gate_kernel,
        grid=(pieces,),
        in_specs=[
            pl.BlockSpec((blocks, 1, share, LANES), lambda a: (0, a, 0, 0)),
            strip,
            strip,
            strip,
            row,
        ],
        out_specs=[strip, pl.BlockSpec((peers, LANES), lambda a: (0, a))],
        out_shape=[
            jax.ShapeDtypeStruct((tokens, channels), F32),
            jax.ShapeDtypeStruct((peers, tokens), F32),
        ],
        compiler_params=params,
        name="gate",
    )(conv, query_gate, key_branch, value_branch, skip_weight[None])
    square = lax.all_to_all(square, "chan", split_axis=0, concat_axis=0, tiled=True)
    return pl.pallas_call(
        norm_kernel,
        grid=(pieces,),
        in_specs=[strip, pl.BlockSpec((peers, LANES), lambda a: (0, a)), row],
        out_specs=strip,
        out_shape=jax.ShapeDtypeStruct((tokens, channels), BF16),
        compiler_params=params,
        name="norm",
    )(gated, square, norm_gain[None])


def solution(mesh):
    wide = P("ctx", "chan")
    return jax.shard_map(
        on_device,
        mesh=mesh,
        in_specs=(wide, wide, wide, wide, P("chan"), P("chan")),
        out_specs=wide,
        check_vma=False,
    )
```

time: 589 us -> 123 us (0.21)
  waiting for transfers between devices: 278 us -> 0 us
  matrix products: 145 us -> 0 us
  starting transfers between devices: 57.4 us -> 0 us
  blocking collectives: 54.3 us -> 108 us
  local copies, waits for them, and re-layouts: 46.9 us -> 3.4 us
  Pallas kernels: 0 us -> 11.6 us
    all_to_all x8 -> x0, waiting for transfers between devices: 278 us -> none  [the longest x1 47.7 us: on_device(): lax.all_to_all(signal_im, 'ctx', split_axis=0, concat_axis=1, tiled=True)]
    dot_general x18 -> x0, matrix products: 145 us -> none  [the longest x12 126 us: along_second(): jnp.einsum('kn,anc->akc', matrix, values, precision=HIGHEST, preferred_el...]
    all_to_all x1 -> x3, blocking collectives: 34.9 us -> 108 us  [the longest x1 62.9 us: on_device(): lax.all_to_all(packed, 'ctx', split_axis=0, concat_axis=0, tiled=True)]
    all_to_all x8 -> x0, starting transfers between devices: 57.4 us -> none  [the longest x1 11.6 us: on_device(): lax.all_to_all(product[None], 'ctx', split_axis=1, concat_axis=0, tiled=T...]
    all_to_all x10 -> x1, local copies, waits for them, and re-layouts: 22 us -> 0.02 us  [on_device(): lax.all_to_all(square, 'chan', split_axis=0, concat_axis=0, tiled=True)]
    psum x1 -> x0, blocking collectives: 19.4 us -> none  [on_device(): total_sq = lax.psum(partial_value, 'chan')]
    pallas_call x0 -> x4, Pallas kernels: none -> 11.6 us  [the longest x1 7.94 us: on_device(): pl.pallas_call(functools.partial(conv_kernel, 4, share), out_shape=jax.Sh...]
    sub x3 -> x0, local copies, waits for them, and re-layouts: 10.9 us -> none  [rotate(): real_part * cosine - imag_part * sine_part]
  transfers between devices with their start and end apart: 8 -> 0, of which waited for: 7 -> 0; matrix products, arithmetic and copies ran while one was open for 15% -> 0% of each run, Pallas kernels for 0% -> 0%
where the time goes in v1:
time: 123 us
  blocking collectives  108 us (88%)
  Pallas kernels  11.6 us (9%)
  local copies, waits for them, and re-layouts  3.4 us (3%)
    all_to_all x1, blocking collectives, on_device(): lax.all_to_all(packed, 'ctx', split_axis=0, concat_axis=0, tiled=True)  62.9 us
    all_to_all x1, blocking collectives, on_device(): conv = lax.all_to_all(conv, 'ctx', split_axis=0, concat_axis=0, tiled=True)  33.9 us
    all_to_all x1, blocking collectives, on_device(): lax.all_to_all(square, 'chan', split_axis=0, concat_axis=0, tiled=True)  11 us
    pallas_call x1, Pallas kernels, on_device(): pl.pallas_call(functools.partial(conv_kernel, 4, share), out_shape=jax.Sh...  7.94 us
    unnamed x29, local copies, waits for them, and re-layouts  3.38 us

profile of v1, /device:TPU:16, one launch (start us, length us, event | category | flops | bytes accessed | tf_op | source)
XLA Modules:
  0.0 122.9 jit_solution(17388057586201121085)
XLA Ops:
  0.0 1.0 copy-done
  1.0 1.0 copy-done.2
  2.1 1.2 copy-done.4
  3.3 1.0 pack.1
  4.3 0.0 copy-start.6
  4.3 0.0 copy-start.7
  4.3 0.0 copy-start.8
  4.3 0.0 copy-start.9
  4.4 0.0 copy-start.10
  4.4 0.0 copy-start.11
  4.4 62.9 %all_to_all.21 = f32[32,128,128]{2,1,0:T(8,128)S(1)} all-to-all(f32[32,128,128]{2,1,0:T(8,128)S(1)} %bitcast.11), channel_id=1, replica_groups=mesh['ctx'=32,'chan'=8] {'ctx'}, dimensions={0} | all-to-all | bytes 4194304 | tf_op jit(solution)/shard_map/all_to_all | solution.py:153
  67.3 0.0 copy-done.8
  67.3 0.0 copy-done.9
  67.3 0.0 copy-done.10
  67.4 7.9 %conv.1 = f32[2048,128]{1,0:T(8,128)S(1)} custom-call(f32[4096,128]{1,0:T(8,128)S(1)} %bitcast.10, bf16[256,384]{1,0:T(8,128)(2,1)S(1)} %copy-done.9, f32[128,128]{1,0:T(8,128)S(1)} %copy-done.11, f32[128,128]{1,0:T(8,128)S(1)} %copy-done.10, bf16[768,256]{1,0:T(8,128)(2,1)S(1)} %copy-done.7, bf16[768,256]{1,0:T(8,128)(2,1)S(1)} %copy-done.6, ...), custom_call_target="tpu_custom_call" | custom-call | tf_op jit(solution)/shard_map/conv/pallas_call | solution.py:156
  75.3 0.0 copy-start.1
  75.3 0.0 copy-start.3
  75.3 0.0 copy-start.5
  75.3 0.0 copy-start.13
  75.3 0.0 copy-start.12
  75.4 33.9 %all_to_all.22 = f32[32,64,128]{2,1,0:T(8,128)S(1)} all-to-all(f32[32,64,128]{2,1,0:T(8,128)S(1)} %bitcast.12), channel_id=1, replica_groups=mesh['ctx'=32,'chan'=8] {'ctx'}, dimensions={0} | all-to-all | bytes 2097152 | tf_op jit(solution)/shard_map/all_to_all | solution.py:163
  109.2 1.0 gate.1
  110.2 11.0 %all_to_all.23 = f32[8,1,512]{2,1,0:T(1,128)S(1)} all-to-all(f32[8,1,512]{2,1,0:T(1,128)S(1)} %copy.13), channel_id=1, replica_groups=mesh['ctx'=32,'chan'=8] {'chan'}, dimensions={0} | all-to-all | bytes 32768 | tf_op jit(solution)/shard_map/all_to_all | solution.py:183
  121.3 1.7 %norm.1 = bf16[512,512]{1,0:T(8,128)(2,1)} custom-call(f32[512,512]{1,0:T(8,128)S(1)} %get-tuple-element.7.gated_ref, f32[8,512]{1,0:T(8,128)S(1)} %bitcast.14, f32[1,512]{1,0:T(1,128)S(1)} %bitcast.16), custom_call_target="tpu_custom_call" | custom-call | tf_op jit(solution)/shard_map/norm/pallas_call | solution.py:184
  (13 shorter events, 0.0 us)
Async XLA Ops:
  0.0 1.0 copy-start
  1.0 1.0 copy-start.2
  2.1 1.2 copy-start.4
  4.3 63.0 %copy-start.6 = (bf16[768,256]{1,0:T(8,128)(2,1)S(1)}, bf16[768,256]{1,0:T(8,128)(2,1)}, u32[]{:S(2)}) copy-start(bf16[768,256]{1,0:T(8,128)(2,1)} %constant.16.clone.back_ref) | copy-start | bytes 1179652
  4.3 63.0 %copy-start.7 = (bf16[768,256]{1,0:T(8,128)(2,1)S(1)}, bf16[768,256]{1,0:T(8,128)(2,1)}, u32[]{:S(2)}) copy-start(bf16[768,256]{1,0:T(8,128)(2,1)} %constant.15.clone.fwd_ref) | copy-start | bytes 1179652
  4.3 63.0 %copy-start.8 = (bf16[128,768]{1,0:T(8,128)(2,1)S(1)}, bf16[128,768]{1,0:T(8,128)(2,1)}, u32[]{:S(2)}) copy-start(bf16[128,768]{1,0:T(8,128)(2,1)} %constant.17.clone.last_ref) | copy-start | bytes 589828
  4.3 63.0 %copy-start.9 = (bf16[256,384]{1,0:T(8,128)(2,1)S(1)}, bf16[256,384]{1,0:T(8,128)(2,1)}, u32[]{:S(2)}) copy-start(bf16[256,384]{1,0:T(8,128)(2,1)} %constant.12.clone.first_ref) | copy-start | bytes 589828
  4.4 63.0 %copy-start.10 = (f32[128,128]{1,0:T(8,128)S(1)}, f32[128,128]{1,0:T(8,128)}, u32[]{:S(2)}) copy-start(f32[128,128]{1,0:T(8,128)} %constant.14.clone.turn_im_ref) | copy-start | bytes 196612
  4.4 63.0 %copy-start.11 = (f32[128,128]{1,0:T(8,128)S(1)}, f32[128,128]{1,0:T(8,128)}, u32[]{:S(2)}) copy-start(f32[128,128]{1,0:T(8,128)} %constant.13.clone.turn_re_ref) | copy-start | bytes 196612
  75.3 33.9 %copy-start.1 = (bf16[512,512]{1,0:T(8,128)(2,1)S(1)}, bf16[512,512]{1,0:T(8,128)(2,1)}, u32[]{:S(2)}) copy-start(bf16[512,512]{1,0:T(8,128)(2,1)} %key_ref.3) | copy-start | bytes 1572868
  75.3 33.9 %copy-start.3 = (bf16[512,512]{1,0:T(8,128)(2,1)S(1)}, bf16[512,512]{1,0:T(8,128)(2,1)}, u32[]{:S(2)}) copy-start(bf16[512,512]{1,0:T(8,128)(2,1)} %value_ref.3) | copy-start | bytes 1572868
  75.3 33.9 %copy-start.5 = (bf16[512,512]{1,0:T(8,128)(2,1)S(1)}, bf16[512,512]{1,0:T(8,128)(2,1)}, u32[]{:S(2)}) copy-start(bf16[512,512]{1,0:T(8,128)(2,1)} %query_ref.1) | copy-start | bytes 1572868
  75.3 33.9 %copy-start.13 = (f32[512]{0:T(512)S(1)}, f32[512]{0:T(512)}, u32[]{:S(2)}) copy-start(f32[512]{0:T(512)} %param.16) | copy-start | bytes 6148
  75.3 45.9 %copy-start.12 = (f32[512]{0:T(512)S(1)}, f32[512]{0:T(512)}, u32[]{:S(2)}) copy-start(f32[512]{0:T(512)} %param.17) | copy-start | bytes 6148

commit v2 on v1

--- a/solution.py
+++ b/solution.py
@@ -15,6 +15,7 @@
 F32 = jnp.float32
 BF16 = jnp.bfloat16
 VMEM_BYTES = 32 * 1024 * 1024
+PACK_VMEM_BYTES = 56 * 1024 * 1024
 
 
 def split_const(values):
@@ -56,11 +57,35 @@
     return jnp.dot(left, right, preferred_element_type=F32)
 
 
-def pack_kernel(key_ref, value_ref, filter_ref, out_ref):
-    share = out_ref.shape[3]
-    product = key_ref[...].astype(F32) * value_ref[...].astype(F32)
-    out_ref[:, 0, 0] = product.T.reshape(-1, share, LANES)
-    out_ref[:, 0, 1] = filter_ref[...].T.reshape(-1, share, LANES)
+def pack_kernel(
+    key_hbm, value_hbm, filter_hbm, out_hbm, key_ref, value_ref, filter_ref, out_ref, sems, out_sems
+):
+    pieces, share = out_ref.shape[1], out_ref.shape[3]
+    pairs = ((key_hbm, key_ref), (value_hbm, value_ref), (filter_hbm, filter_ref))
+    copies = []
+    for piece in range(pieces):
+        at = pl.ds(piece * LANES, LANES)
+        for index, (source, target) in enumerate(pairs):
+            copies.append(
+                pltpu.make_async_copy(source.at[at], target.at[at], sems.at[piece, index])
+            )
+    for copy in copies:
+        copy.start()
+    sends = []
+    for piece in range(pieces):
+        at = pl.ds(piece * LANES, LANES)
+        copies[3 * piece].wait()
+        copies[3 * piece + 1].wait()
+        product = key_ref[at, :].astype(F32) * value_ref[at, :].astype(F32)
+        out_ref[:, piece, 0] = product.T.reshape(-1, share, LANES)
+        copies[3 * piece + 2].wait()
+        out_ref[:, piece, 1] = filter_ref[at, :].T.reshape(-1, share, LANES)
+        sends.append(
+            pltpu.make_async_copy(out_ref.at[:, piece], out_hbm.at[:, piece], out_sems.at[piece])
+        )
+        sends[-1].start()
+    for send in sends:
+        send.wait()
 
 
 def conv_kernel(
@@ -69,20 +94,30 @@
     rows = turn_re_ref.shape[0]
     turn_re = jnp.concatenate([turn_re_ref[...]] * 2, axis=1)
     turn_im = jnp.concatenate([turn_im_ref[...]] * 2, axis=1)
-    for start in range(0, share, group):
+
+    def over_rows(table_ref, values):
+        high, low = split(values)
+        return dot(table_ref[...], jnp.concatenate([high, low, high], axis=0))
+
+    def over_lanes(values, table_ref):
+        high, low = split(values)
+        return dot(jnp.concatenate([high, low, high], axis=1), table_ref[...])
+
+    def first_stage(start):
         parts = []
         for c in range(start, start + group):
             signal = data_ref[pl.ds(c, rows, stride=2 * share), :]
             kernel = data_ref[pl.ds(share + c, rows, stride=2 * share), :]
-            high, low = split(jnp.concatenate([signal, kernel], axis=1))
-            spec = dot(first_ref[...], jnp.concatenate([high, low, high], axis=0))
+            spec = over_rows(first_ref, jnp.concatenate([signal, kernel], axis=1))
             re, im = spec[:rows], spec[rows:]
             out_re = re * turn_re - im * turn_im
             out_im = re * turn_im + im * turn_re
             parts.append(jnp.concatenate([out_re[:, :LANES], out_im[:, :LANES]], axis=1))
             parts.append(jnp.concatenate([out_re[:, LANES:], out_im[:, LANES:]], axis=1))
-        high, low = split(jnp.concatenate(parts, axis=0))
-        spec = dot(jnp.concatenate([high, low, high], axis=1), fwd_ref[...])
+        return jnp.concatenate(parts, axis=0)
+
+    def product_of_spectra(turned):
+        spec = over_lanes(turned, fwd_ref)
         parts = []
         for c in range(group):
             signal = spec[2 * c * rows : (2 * c + 1) * rows]
@@ -92,8 +127,9 @@
             parts.append(
                 jnp.concatenate([s_re * k_re - s_im * k_im, s_re * k_im + s_im * k_re], axis=1)
             )
-        high, low = split(jnp.concatenate(parts, axis=0))
-        spec = dot(jnp.concatenate([high, low, high], axis=1), back_ref[...])
+        return jnp.concatenate(parts, axis=0)
+
+    def last_stage(spec, start):
         for c in range(0, group, 2):
             first = spec[c * rows : (c + 1) * rows]
             second = spec[(c + 1) * rows : (c + 2) * rows]
@@ -102,10 +138,21 @@
             turned = jnp.concatenate(
                 [re * turn_re + im * turn_im, im * turn_re - re * turn_im], axis=0
             )
-            high, low = split(turned)
-            conv = dot(last_ref[...], jnp.concatenate([high, low, high], axis=0))
+            conv = over_rows(last_ref, turned)
             out_ref[pl.ds(start + c, rows, stride=share), :] = conv[:, :LANES]
             out_ref[pl.ds(start + c + 1, rows, stride=share), :] = conv[:, LANES:]
+
+    groups = share // group
+    turned, spectra, back = {}, {}, {}
+    for step in range(groups + 3):
+        if step < groups:
+            turned[step] = first_stage(step * group)
+        if 0 <= step - 1 < groups:
+            spectra[step - 1] = product_of_spectra(turned.pop(step - 1))
+        if 0 <= step - 2 < groups:
+            back[step - 2] = over_lanes(spectra.pop(step - 2), back_ref)
+        if 0 <= step - 3 < groups:
+            last_stage(back.pop(step - 3), (step - 3) * group)
 
 
 def gate_kernel(conv_ref, query_ref, key_ref, value_ref, skip_ref, gated_ref, square_ref):
@@ -124,10 +171,12 @@
 def norm_kernel(gated_ref, square_ref, gain_ref, out_ref):
     total = jnp.sum(square_ref[...], axis=0, keepdims=True)
     inverse = lax.rsqrt(total / CH + 1e-05)
-    spread = jnp.broadcast_to(inverse, (LANES, LANES)).T
-    for start in range(0, out_ref.shape[1], LANES):
-        at = slice(start, start + LANES)
-        out_ref[:, at] = (gated_ref[:, at] * spread * gain_ref[:, at]).astype(BF16)
+    for top in range(0, out_ref.shape[0], LANES):
+        down = slice(top, top + LANES)
+        spread = jnp.broadcast_to(inverse[:, down], (LANES, LANES)).T
+        for start in range(0, out_ref.shape[1], LANES):
+            at = slice(start, start + LANES)
+            out_ref[down, at] = (gated_ref[down, at] * spread * gain_ref[:, at]).astype(BF16)
 
 
 def on_device(query_gate, key_branch, value_branch, conv_filter, skip_weight, norm_gain):
@@ -140,13 +189,23 @@
     params = pltpu.CompilerParams(vmem_limit_bytes=VMEM_BYTES)
     strip = pl.BlockSpec((LANES, channels), lambda a: (a, 0))
     row = pl.BlockSpec((1, channels), lambda a: (0, 0))
+    whole = (tokens, channels)
+    whole = (tokens, channels)
+    packed_shape = (blocks, pieces, 2, share, LANES)
     packed = pl.pallas_call(
         pack_kernel,
-        grid=(pieces,),
-        in_specs=[strip] * 3,
-        out_specs=pl.BlockSpec((blocks, 1, 2, share, LANES), lambda a: (0, a, 0, 0, 0)),
-        out_shape=jax.ShapeDtypeStruct((blocks, pieces, 2, share, LANES), F32),
-        compiler_params=params,
+        in_specs=[pl.BlockSpec(memory_space=pltpu.HBM)] * 3,
+        out_specs=pl.BlockSpec(memory_space=pltpu.HBM),
+        out_shape=jax.ShapeDtypeStruct(packed_shape, F32),
+        scratch_shapes=[
+            pltpu.VMEM(whole, BF16),
+            pltpu.VMEM(whole, BF16),
+            pltpu.VMEM(whole, F32),
+            pltpu.VMEM(packed_shape, F32),
+            pltpu.SemaphoreType.DMA((pieces, 3)),
+            pltpu.SemaphoreType.DMA((pieces,)),
+        ],
+        compiler_params=pltpu.CompilerParams(vmem_limit_bytes=PACK_VMEM_BYTES),
         name="pack",
     )(key_branch, value_branch, conv_filter)
     packed = packed.reshape(blocks, pieces * 2 * share, LANES)
@@ -183,9 +242,6 @@
     square = lax.all_to_all(square, "chan", split_axis=0, concat_axis=0, tiled=True)
     return pl.pallas_call(
         norm_kernel,
-        grid=(pieces,),
-        in_specs=[strip, pl.BlockSpec((peers, LANES), lambda a: (0, a)), row],
-        out_specs=strip,
         out_shape=jax.ShapeDtypeStruct((tokens, channels), BF16),
         compiler_params=params,
         name="norm",

time: 123 us -> 119 us (0.967)
  local copies, waits for them, and re-layouts: 3.4 us -> 0.09 us
  Pallas kernels: 11.6 us -> 10.3 us
    unnamed x29 -> x23, local copies, waits for them, and re-layouts: 3.38 us -> 0.07 us
    pallas_call x1, Pallas kernels: 7.94 us -> 5.36 us  [on_device(): pl.pallas_call(functools.partial(conv_kernel, 4, share), out_shape=jax.Sh...]
    pallas_call x2, Pallas kernels: 2.67 us -> 4.02 us  [the longest x1 3.03 us: on_device(): pl.pallas_call(pack_kernel, in_specs=[pl.BlockSpec(memory_space=pltpu.HBM...]
where the time goes in v2:
time: 119 us
  blocking collectives  108 us (91%)
  Pallas kernels  10.3 us (9%)
    all_to_all x1, blocking collectives, on_device(): lax.all_to_all(packed, 'ctx', split_axis=0, concat_axis=0, tiled=True)  63.1 us
    all_to_all x1, blocking collectives, on_device(): conv = lax.all_to_all(conv, 'ctx', split_axis=0, concat_axis=0, tiled=True)  33.9 us
    all_to_all x1, blocking collectives, on_device(): lax.all_to_all(square, 'chan', split_axis=0, concat_axis=0, tiled=True)  11 us
    pallas_call x1, Pallas kernels, on_device(): pl.pallas_call(functools.partial(conv_kernel, 4, share), out_shape=jax.Sh...  5.36 us
    pallas_call x1, Pallas kernels, on_device(): pl.pallas_call(pack_kernel, in_specs=[pl.BlockSpec(memory_space=pltpu.HBM...  3.03 us

profile of v2, /device:TPU:16, one launch (start us, length us, event | category | flops | bytes accessed | tf_op | source)
XLA Modules:
  0.0 118.6 jit_solution(17724648561197335724)
XLA Ops:
  0.0 3.0 %pack.1 = f32[32,4,2,16,128]{4,3,2,1,0:T(8,128)} custom-call(bf16[512,512]{1,0:T(8,128)(2,1)} %key_ref.1, bf16[512,512]{1,0:T(8,128)(2,1)} %value_ref.1, f32[512,512]{1,0:T(8,128)} %filter_hbm.1), custom_call_target="tpu_custom_call" | custom-call | tf_op jit(solution)/shard_map/pack/pallas_call | solution.py:195
  3.0 0.0 copy-start.3
  3.0 0.0 copy-start.4
  3.1 0.0 copy-start.5
  3.1 0.0 copy-start.6
  3.1 0.0 copy-start.7
  3.1 0.0 copy-start.8
  3.1 63.1 %all_to_all.21 = f32[32,128,128]{2,1,0:T(8,128)S(1)} all-to-all(f32[32,128,128]{2,1,0:T(8,128)} %bitcast.17), channel_id=1, replica_groups=mesh['ctx'=32,'chan'=8] {'ctx'}, dimensions={0} | all-to-all | bytes 4194304 | tf_op jit(solution)/shard_map/all_to_all | solution.py:212
  66.2 0.0 copy-done.3
  66.3 0.0 copy-done.4
  66.3 0.0 copy-done.5
  66.3 0.0 copy-done.6
  66.3 0.0 copy-done.7
  66.3 5.4 %conv.1 = f32[2048,128]{1,0:T(8,128)S(1)} custom-call(f32[4096,128]{1,0:T(8,128)S(1)} %bitcast.10, bf16[256,384]{1,0:T(8,128)(2,1)S(1)} %copy-done.6, f32[128,128]{1,0:T(8,128)S(1)} %copy-done.8, f32[128,128]{1,0:T(8,128)S(1)} %copy-done.7, bf16[768,256]{1,0:T(8,128)(2,1)S(1)} %copy-done.4, bf16[768,256]{1,0:T(8,128)(2,1)S(1)} %copy-done.3, ...), custom_call_target="tpu_custom_call" | custom-call | tf_op jit(solution)/shard_map/conv/pallas_call | solution.py:215
  71.7 0.0 copy-start
  71.7 0.0 copy-start.1
  71.7 0.0 copy-start.2
  71.7 0.0 copy-start.10
  71.7 0.0 copy-start.9
  71.7 33.9 %all_to_all.22 = f32[32,64,128]{2,1,0:T(8,128)S(1)} all-to-all(f32[32,64,128]{2,1,0:T(8,128)S(1)} %bitcast.11), channel_id=1, replica_groups=mesh['ctx'=32,'chan'=8] {'ctx'}, dimensions={0} | all-to-all | bytes 2097152 | tf_op jit(solution)/shard_map/all_to_all | solution.py:222
  105.6 0.0 copy-done.10
  105.6 1.0 gate.1
  106.6 11.0 %all_to_all.23 = f32[8,1,512]{2,1,0:T(1,128)S(1)} all-to-all(f32[8,1,512]{2,1,0:T(1,128)S(1)} %copy.13), channel_id=1, replica_groups=mesh['ctx'=32,'chan'=8] {'chan'}, dimensions={0} | all-to-all | bytes 32768 | tf_op jit(solution)/shard_map/all_to_all | solution.py:242
  117.6 1.0 norm.1
  (7 shorter events, 0.0 us)
Async XLA Ops:
  3.0 63.2 %copy-start.3 = (bf16[768,256]{1,0:T(8,128)(2,1)S(1)}, bf16[768,256]{1,0:T(8,128)(2,1)}, u32[]{:S(2)}) copy-start(bf16[768,256]{1,0:T(8,128)(2,1)} %constant.16.clone.back_ref) | copy-start | bytes 1179652
  3.0 63.2 %copy-start.4 = (bf16[768,256]{1,0:T(8,128)(2,1)S(1)}, bf16[768,256]{1,0:T(8,128)(2,1)}, u32[]{:S(2)}) copy-start(bf16[768,256]{1,0:T(8,128)(2,1)} %constant.15.clone.fwd_ref) | copy-start | bytes 1179652
  3.1 63.2 %copy-start.5 = (bf16[128,768]{1,0:T(8,128)(2,1)S(1)}, bf16[128,768]{1,0:T(8,128)(2,1)}, u32[]{:S(2)}) copy-start(bf16[128,768]{1,0:T(8,128)(2,1)} %constant.17.clone.last_ref) | copy-start | bytes 589828
  3.1 63.2 %copy-start.6 = (bf16[256,384]{1,0:T(8,128)(2,1)S(1)}, bf16[256,384]{1,0:T(8,128)(2,1)}, u32[]{:S(2)}) copy-start(bf16[256,384]{1,0:T(8,128)(2,1)} %constant.12.clone.first_ref) | copy-start | bytes 589828
  3.1 63.2 %copy-start.7 = (f32[128,128]{1,0:T(8,128)S(1)}, f32[128,128]{1,0:T(8,128)}, u32[]{:S(2)}) copy-start(f32[128,128]{1,0:T(8,128)} %constant.14.clone.turn_im_ref) | copy-start | bytes 196612
  3.1 63.2 %copy-start.8 = (f32[128,128]{1,0:T(8,128)S(1)}, f32[128,128]{1,0:T(8,128)}, u32[]{:S(2)}) copy-start(f32[128,128]{1,0:T(8,128)} %constant.13.clone.turn_re_ref) | copy-start | bytes 196612
  71.7 33.9 %copy-start = (bf16[512,512]{1,0:T(8,128)(2,1)S(1)}, bf16[512,512]{1,0:T(8,128)(2,1)}, u32[]{:S(2)}) copy-start(bf16[512,512]{1,0:T(8,128)(2,1)} %key_ref.1) | copy-start | bytes 1572868
  71.7 33.9 %copy-start.1 = (bf16[512,512]{1,0:T(8,128)(2,1)S(1)}, bf16[512,512]{1,0:T(8,128)(2,1)}, u32[]{:S(2)}) copy-start(bf16[512,512]{1,0:T(8,128)(2,1)} %value_ref.1) | copy-start | bytes 1572868
  71.7 33.9 %copy-start.2 = (bf16[512,512]{1,0:T(8,128)(2,1)S(1)}, bf16[512,512]{1,0:T(8,128)(2,1)}, u32[]{:S(2)}) copy-start(bf16[512,512]{1,0:T(8,128)(2,1)} %query_ref.1) | copy-start | bytes 1572868
  71.7 33.9 %copy-start.10 = (f32[512]{0:T(512)S(1)}, f32[512]{0:T(512)}, u32[]{:S(2)}) copy-start(f32[512]{0:T(512)} %param.16) | copy-start | bytes 6148
  71.7 45.9 %copy-start.9 = (f32[512]{0:T(512)S(1)}, f32[512]{0:T(512)}, u32[]{:S(2)}) copy-start(f32[512]{0:T(512)} %param.17) | copy-start | bytes 6148

commit v3 on v2

--- a/solution.py
+++ b/solution.py
@@ -30,7 +30,7 @@
     b = np.arange(cols, dtype=np.float64)
     first = 2.0 * math.pi * np.outer(m + 0.25, m) / rows
     first_high, first_low = split_const(np.concatenate([np.cos(first), -np.sin(first)], axis=0))
-    first_table = np.concatenate([first_high, first_high, first_low], axis=1)
+    first_table = np.block([[first_high, first_high], [first_low, np.zeros_like(first_low)]])
     turn = 2.0 * math.pi * np.outer(m + 0.25, b) / length
     turn_re = np.cos(turn).astype(np.float32)
     turn_im = (-np.sin(turn)).astype(np.float32)
@@ -43,7 +43,7 @@
     last_high, last_low = split_const(
         np.concatenate([np.cos(first.T), -np.sin(first.T)], axis=1) / length
     )
-    last_table = np.concatenate([last_high, last_high, last_low], axis=1)
+    last_table = np.concatenate([last_high, last_low], axis=0)
     return first_table, turn_re, turn_im, fwd_table, back_table, last_table
 
 
@@ -72,20 +72,29 @@
     for copy in copies:
         copy.start()
     sends = []
+
+    def send(piece, stream):
+        sends.append(
+            pltpu.make_async_copy(
+                out_ref.at[:, piece, stream],
+                out_hbm.at[:, piece, stream],
+                out_sems.at[piece, stream],
+            )
+        )
+        sends[-1].start()
+
     for piece in range(pieces):
         at = pl.ds(piece * LANES, LANES)
         copies[3 * piece].wait()
         copies[3 * piece + 1].wait()
         product = key_ref[at, :].astype(F32) * value_ref[at, :].astype(F32)
         out_ref[:, piece, 0] = product.T.reshape(-1, share, LANES)
+        send(piece, 0)
         copies[3 * piece + 2].wait()
         out_ref[:, piece, 1] = filter_ref[at, :].T.reshape(-1, share, LANES)
-        sends.append(
-            pltpu.make_async_copy(out_ref.at[:, piece], out_hbm.at[:, piece], out_sems.at[piece])
-        )
-        sends[-1].start()
-    for send in sends:
-        send.wait()
+        send(piece, 1)
+    for copy in sends:
+        copy.wait()
 
 
 def conv_kernel(
@@ -95,10 +104,6 @@
     turn_re = jnp.concatenate([turn_re_ref[...]] * 2, axis=1)
     turn_im = jnp.concatenate([turn_im_ref[...]] * 2, axis=1)
 
-    def over_rows(table_ref, values):
-        high, low = split(values)
-        return dot(table_ref[...], jnp.concatenate([high, low, high], axis=0))
-
     def over_lanes(values, table_ref):
         high, low = split(values)
         return dot(jnp.concatenate([high, low, high], axis=1), table_ref[...])
@@ -108,8 +113,10 @@
         for c in range(start, start + group):
             signal = data_ref[pl.ds(c, rows, stride=2 * share), :]
             kernel = data_ref[pl.ds(share + c, rows, stride=2 * share), :]
-            spec = over_rows(first_ref, jnp.concatenate([signal, kernel], axis=1))
-            re, im = spec[:rows], spec[rows:]
+            high, low = split(jnp.concatenate([signal, kernel], axis=1))
+            spec = dot(first_ref[...], jnp.concatenate([high, low], axis=0))
+            re = spec[:rows] + spec[2 * rows : 3 * rows]
+            im = spec[rows : 2 * rows] + spec[3 * rows :]
             out_re = re * turn_re - im * turn_im
             out_im = re * turn_im + im * turn_re
             parts.append(jnp.concatenate([out_re[:, :LANES], out_im[:, :LANES]], axis=1))
@@ -138,34 +145,38 @@
             turned = jnp.concatenate(
                 [re * turn_re + im * turn_im, im * turn_re - re * turn_im], axis=0
             )
-            conv = over_rows(last_ref, turned)
+            high, low = split(turned)
+            conv = dot(last_ref[...], high)
+            conv = conv[:rows] + dot(last_ref[:rows], low) + conv[rows:]
             out_ref[pl.ds(start + c, rows, stride=share), :] = conv[:, :LANES]
             out_ref[pl.ds(start + c + 1, rows, stride=share), :] = conv[:, LANES:]
 
     groups = share // group
     turned, spectra, back = {}, {}, {}
     for step in range(groups + 3):
+        if 0 <= step - 1 < groups:
+            spectra[step - 1] = product_of_spectra(turned.pop(step - 1))
         if step < groups:
             turned[step] = first_stage(step * group)
-        if 0 <= step - 1 < groups:
-            spectra[step - 1] = product_of_spectra(turned.pop(step - 1))
+        if 0 <= step - 3 < groups:
+            last_stage(back.pop(step - 3), (step - 3) * group)
         if 0 <= step - 2 < groups:
             back[step - 2] = over_lanes(spectra.pop(step - 2), back_ref)
-        if 0 <= step - 3 < groups:
-            last_stage(back.pop(step - 3), (step - 3) * group)
 
 
 def gate_kernel(conv_ref, query_ref, key_ref, value_ref, skip_ref, gated_ref, square_ref):
-    conv = conv_ref[...].reshape(-1, LANES).T
-    product = key_ref[...].astype(F32) * value_ref[...].astype(F32)
-    gated = query_ref[...].astype(F32) * (conv + skip_ref[...] * product)
-    gated_ref[...] = gated
-    square = gated * gated
-    folded = square[:, :LANES]
-    for start in range(LANES, square.shape[1], LANES):
-        folded = folded + square[:, start : start + LANES]
-    total = jnp.sum(folded.T, axis=0, keepdims=True)
-    square_ref[...] = jnp.broadcast_to(total, square_ref.shape)
+    for piece in range(conv_ref.shape[1]):
+        at = slice(piece * LANES, (piece + 1) * LANES)
+        conv = conv_ref[:, piece].reshape(-1, LANES).T
+        product = key_ref[at, :].astype(F32) * value_ref[at, :].astype(F32)
+        gated = query_ref[at, :].astype(F32) * (conv + skip_ref[...] * product)
+        gated_ref[at, :] = gated
+        square = gated * gated
+        folded = square[:, :LANES]
+        for start in range(LANES, square.shape[1], LANES):
+            folded = folded + square[:, start : start + LANES]
+        total = jnp.sum(folded.T, axis=0, keepdims=True)
+        square_ref[:, at] = jnp.broadcast_to(total, (square_ref.shape[0], LANES))
 
 
 def norm_kernel(gated_ref, square_ref, gain_ref, out_ref):
@@ -203,7 +214,7 @@
             pltpu.VMEM(whole, F32),
             pltpu.VMEM(packed_shape, F32),
             pltpu.SemaphoreType.DMA((pieces, 3)),
-            pltpu.SemaphoreType.DMA((pieces,)),
+            pltpu.SemaphoreType.DMA((pieces, 2)),
         ],
         compiler_params=pltpu.CompilerParams(vmem_limit_bytes=PACK_VMEM_BYTES),
         name="pack",
@@ -223,15 +234,6 @@
     conv = conv.reshape(blocks, pieces, share, LANES)
     gated, square = pl.pallas_call(
         gate_kernel,
-        grid=(pieces,),
-        in_specs=[
-            pl.BlockSpec((blocks, 1, share, LANES), lambda a: (0, a, 0, 0)),
-            strip,
-            strip,
-            strip,
-            row,
-        ],
-        out_specs=[strip, pl.BlockSpec((peers, LANES), lambda a: (0, a))],
         out_shape=[
             jax.ShapeDtypeStruct((tokens, channels), F32),
             jax.ShapeDtypeStruct((peers, tokens), F32),

time: 119 us -> 118 us (level)
  no operation moved by 1% of the time
where the time goes in v3:
time: 118 us
  blocking collectives  108 us (92%)
  Pallas kernels  9.73 us (8%)
    all_to_all x1, blocking collectives, on_device(): lax.all_to_all(packed, 'ctx', split_axis=0, concat_axis=0, tiled=True)  63.1 us
    all_to_all x1, blocking collectives, on_device(): conv = lax.all_to_all(conv, 'ctx', split_axis=0, concat_axis=0, tiled=True)  33.9 us
    all_to_all x1, blocking collectives, on_device(): lax.all_to_all(square, 'chan', split_axis=0, concat_axis=0, tiled=True)  11 us
    pallas_call x1, Pallas kernels, on_device(): pl.pallas_call(functools.partial(conv_kernel, 4, share), out_shape=jax.Sh...  5.13 us
    pallas_call x1, Pallas kernels, on_device(): pl.pallas_call(pack_kernel, in_specs=[pl.BlockSpec(memory_space=pltpu.HBM...  2.97 us

profile of v3, /device:TPU:16, one launch (start us, length us, event | category | flops | bytes accessed | tf_op | source)
XLA Modules:
  0.0 118.0 jit_solution(18132902294408121508)
XLA Ops:
  0.0 3.0 %pack.1 = f32[32,4,2,16,128]{4,3,2,1,0:T(8,128)} custom-call(bf16[512,512]{1,0:T(8,128)(2,1)} %key_ref.1, bf16[512,512]{1,0:T(8,128)(2,1)} %value_ref.1, f32[512,512]{1,0:T(8,128)} %filter_hbm.1), custom_call_target="tpu_custom_call" | custom-call | tf_op jit(solution)/shard_map/pack/pallas_call | solution.py:206
  3.0 0.0 copy-start.3
  3.0 0.0 copy-start.4
  3.0 0.0 copy-start.5
  3.0 0.0 copy-start.6
  3.0 0.0 copy-start.7
  3.0 0.0 copy-start.8
  3.1 63.1 %all_to_all.21 = f32[32,128,128]{2,1,0:T(8,128)S(1)} all-to-all(f32[32,128,128]{2,1,0:T(8,128)} %bitcast.17), channel_id=1, replica_groups=mesh['ctx'=32,'chan'=8] {'ctx'}, dimensions={0} | all-to-all | bytes 4194304 | tf_op jit(solution)/shard_map/all_to_all | solution.py:223
  66.2 0.0 copy-done.3
  66.2 0.0 copy-done.5
  66.2 0.0 copy-done.6
  66.2 0.0 copy-done.7
  66.2 0.0 copy-done.8
  66.2 5.1 %conv.1 = f32[2048,128]{1,0:T(8,128)S(1)} custom-call(f32[4096,128]{1,0:T(8,128)S(1)} %bitcast.10, bf16[512,256]{1,0:T(8,128)(2,1)S(1)} %copy-done.5, f32[128,128]{1,0:T(8,128)S(1)} %copy-done.8, f32[128,128]{1,0:T(8,128)S(1)} %copy-done.7, bf16[768,256]{1,0:T(8,128)(2,1)S(1)} %copy-done.4, bf16[768,256]{1,0:T(8,128)(2,1)S(1)} %copy-done.3, ...), custom_call_target="tpu_custom_call" | custom-call | tf_op jit(solution)/shard_map/conv/pallas_call | solution.py:226
  71.4 0.0 copy-start
  71.4 0.0 copy-start.1
  71.4 0.0 copy-start.2
  71.4 0.0 copy-start.10
  71.4 0.0 copy-start.9
  71.4 33.9 %all_to_all.22 = f32[32,64,128]{2,1,0:T(8,128)S(1)} all-to-all(f32[32,64,128]{2,1,0:T(8,128)S(1)} %bitcast.11), channel_id=1, replica_groups=mesh['ctx'=32,'chan'=8] {'ctx'}, dimensions={0} | all-to-all | bytes 2097152 | tf_op jit(solution)/shard_map/all_to_all | solution.py:233
  105.3 0.0 copy-done
  105.3 0.6 gate.1
  106.0 11.0 %all_to_all.23 = f32[8,1,512]{2,1,0:T(1,128)S(1)} all-to-all(f32[8,1,512]{2,1,0:T(1,128)S(1)} %copy.13), channel_id=1, replica_groups=mesh['ctx'=32,'chan'=8] {'chan'}, dimensions={0} | all-to-all | bytes 32768 | tf_op jit(solution)/shard_map/all_to_all | solution.py:244
  117.0 1.0 norm.1
  (7 shorter events, 0.0 us)
Async XLA Ops:
  3.0 63.2 %copy-start.3 = (bf16[768,256]{1,0:T(8,128)(2,1)S(1)}, bf16[768,256]{1,0:T(8,128)(2,1)}, u32[]{:S(2)}) copy-start(bf16[768,256]{1,0:T(8,128)(2,1)} %constant.16.clone.back_ref) | copy-start | bytes 1179652
  3.0 63.2 %copy-start.4 = (bf16[768,256]{1,0:T(8,128)(2,1)S(1)}, bf16[768,256]{1,0:T(8,128)(2,1)}, u32[]{:S(2)}) copy-start(bf16[768,256]{1,0:T(8,128)(2,1)} %constant.15.clone.fwd_ref) | copy-start | bytes 1179652
  3.0 63.2 %copy-start.5 = (bf16[512,256]{1,0:T(8,128)(2,1)S(1)}, bf16[512,256]{1,0:T(8,128)(2,1)}, u32[]{:S(2)}) copy-start(bf16[512,256]{1,0:T(8,128)(2,1)} %constant.12.clone.first_ref) | copy-start | bytes 786436
  3.0 63.2 %copy-start.6 = (bf16[256,256]{1,0:T(8,128)(2,1)S(1)}, bf16[256,256]{1,0:T(8,128)(2,1)}, u32[]{:S(2)}) copy-start(bf16[256,256]{1,0:T(8,128)(2,1)} %constant.17.clone.last_ref) | copy-start | bytes 393220
  3.0 63.2 %copy-start.7 = (f32[128,128]{1,0:T(8,128)S(1)}, f32[128,128]{1,0:T(8,128)}, u32[]{:S(2)}) copy-start(f32[128,128]{1,0:T(8,128)} %constant.14.clone.turn_im_ref) | copy-start | bytes 196612
  3.0 63.2 %copy-start.8 = (f32[128,128]{1,0:T(8,128)S(1)}, f32[128,128]{1,0:T(8,128)}, u32[]{:S(2)}) copy-start(f32[128,128]{1,0:T(8,128)} %constant.13.clone.turn_re_ref) | copy-start | bytes 196612
  71.4 33.9 %copy-start = (bf16[512,512]{1,0:T(8,128)(2,1)S(1)}, bf16[512,512]{1,0:T(8,128)(2,1)}, u32[]{:S(2)}) copy-start(bf16[512,512]{1,0:T(8,128)(2,1)} %key_ref.1) | copy-start | bytes 1572868
  71.4 33.9 %copy-start.1 = (bf16[512,512]{1,0:T(8,128)(2,1)S(1)}, bf16[512,512]{1,0:T(8,128)(2,1)}, u32[]{:S(2)}) copy-start(bf16[512,512]{1,0:T(8,128)(2,1)} %value_ref.1) | copy-start | bytes 1572868
  71.4 33.9 %copy-start.2 = (bf16[512,512]{1,0:T(8,128)(2,1)S(1)}, bf16[512,512]{1,0:T(8,128)(2,1)}, u32[]{:S(2)}) copy-start(bf16[512,512]{1,0:T(8,128)(2,1)} %query_ref.1) | copy-start | bytes 1572868
  71.4 33.9 %copy-start.10 = (f32[512]{0:T(512)S(1)}, f32[512]{0:T(512)}, u32[]{:S(2)}) copy-start(f32[512]{0:T(512)} %param.16) | copy-start | bytes 6148
  71.4 45.6 %copy-start.9 = (f32[512]{0:T(512)S(1)}, f32[512]{0:T(512)}, u32[]{:S(2)}) copy-start(f32[512]{0:T(512)} %param.17) | copy-start | bytes 6148

commit v4 on v3

--- a/solution.py
+++ b/solution.py
@@ -15,7 +15,6 @@
 F32 = jnp.float32
 BF16 = jnp.bfloat16
 VMEM_BYTES = 32 * 1024 * 1024
-PACK_VMEM_BYTES = 56 * 1024 * 1024
 
 
 def split_const(values):
@@ -57,44 +56,29 @@
     return jnp.dot(left, right, preferred_element_type=F32)
 
 
-def pack_kernel(
-    key_hbm, value_hbm, filter_hbm, out_hbm, key_ref, value_ref, filter_ref, out_ref, sems, out_sems
-):
+def pack_kernel(key_hbm, value_hbm, filter_hbm, out_ref, key_ref, value_ref, filter_ref, sems):
     pieces, share = out_ref.shape[1], out_ref.shape[3]
+    half = pieces // 2
     pairs = ((key_hbm, key_ref), (value_hbm, value_ref), (filter_hbm, filter_ref))
     copies = []
-    for piece in range(pieces):
-        at = pl.ds(piece * LANES, LANES)
+    for part in range(2):
+        at = pl.ds(part * half * LANES, half * LANES)
         for index, (source, target) in enumerate(pairs):
             copies.append(
-                pltpu.make_async_copy(source.at[at], target.at[at], sems.at[piece, index])
+                pltpu.make_async_copy(source.at[at], target.at[at], sems.at[part, index])
             )
     for copy in copies:
         copy.start()
-    sends = []
-
-    def send(piece, stream):
-        sends.append(
-            pltpu.make_async_copy(
-                out_ref.at[:, piece, stream],
-                out_hbm.at[:, piece, stream],
-                out_sems.at[piece, stream],
-            )
-        )
-        sends[-1].start()
-
     for piece in range(pieces):
         at = pl.ds(piece * LANES, LANES)
-        copies[3 * piece].wait()
-        copies[3 * piece + 1].wait()
+        if piece % half == 0:
+            copies[3 * (piece // half)].wait()
+            copies[3 * (piece // half) + 1].wait()
         product = key_ref[at, :].astype(F32) * value_ref[at, :].astype(F32)
         out_ref[:, piece, 0] = product.T.reshape(-1, share, LANES)
-        send(piece, 0)
-        copies[3 * piece + 2].wait()
+        if piece % half == 0:
+            copies[3 * (piece // half) + 2].wait()
         out_ref[:, piece, 1] = filter_ref[at, :].T.reshape(-1, share, LANES)
-        send(piece, 1)
-    for copy in sends:
-        copy.wait()
 
 
 def conv_kernel(
@@ -203,22 +187,24 @@
     whole = (tokens, channels)
     whole = (tokens, channels)
     packed_shape = (blocks, pieces, 2, share, LANES)
+    inputs = [
+        pltpu.with_memory_space_constraint(array, pltpu.HBM)
+        for array in (key_branch, value_branch, conv_filter)
+    ]
     packed = pl.pallas_call(
         pack_kernel,
         in_specs=[pl.BlockSpec(memory_space=pltpu.HBM)] * 3,
-        out_specs=pl.BlockSpec(memory_space=pltpu.HBM),
+        out_specs=pl.BlockSpec(memory_space=pltpu.VMEM),
         out_shape=jax.ShapeDtypeStruct(packed_shape, F32),
         scratch_shapes=[
             pltpu.VMEM(whole, BF16),
             pltpu.VMEM(whole, BF16),
             pltpu.VMEM(whole, F32),
-            pltpu.VMEM(packed_shape, F32),
-            pltpu.SemaphoreType.DMA((pieces, 3)),
-            pltpu.SemaphoreType.DMA((pieces, 2)),
+            pltpu.SemaphoreType.DMA((2, 3)),
         ],
-        compiler_params=pltpu.CompilerParams(vmem_limit_bytes=PACK_VMEM_BYTES),
+        compiler_params=params,
         name="pack",
-    )(key_branch, value_branch, conv_filter)
+    )(*inputs)
     packed = packed.reshape(blocks, pieces * 2 * share, LANES)
     gathered = lax.all_to_all(packed, "ctx", split_axis=0, concat_axis=0, tiled=True)
     gathered = gathered.reshape(rows * 2 * share, LANES)

time: 118 us -> 117 us (level)
  no operation moved by 1% of the time
where the time goes in v4:
time: 117 us
  blocking collectives  108 us (92%)
  Pallas kernels  8.69 us (7%)
    all_to_all x1, blocking collectives, on_device(): lax.all_to_all(packed, 'ctx', split_axis=0, concat_axis=0, tiled=True)  62.9 us
    all_to_all x1, blocking collectives, on_device(): conv = lax.all_to_all(conv, 'ctx', split_axis=0, concat_axis=0, tiled=True)  33.9 us
    all_to_all x1, blocking collectives, on_device(): lax.all_to_all(square, 'chan', split_axis=0, concat_axis=0, tiled=True)  11 us
    pallas_call x1, Pallas kernels, on_device(): pl.pallas_call(functools.partial(conv_kernel, 4, share), out_shape=jax.Sh...  5.13 us

profile of v4, /device:TPU:16, one launch (start us, length us, event | category | flops | bytes accessed | tf_op | source)
XLA Modules:
  0.0 116.7 jit_solution(11085122960273919393)
XLA Ops:
  0.0 1.9 %pack.1 = f32[32,4,2,16,128]{4,3,2,1,0:T(8,128)S(1)} custom-call(bf16[512,512]{1,0:T(8,128)(2,1)} %key_ref.1, bf16[512,512]{1,0:T(8,128)(2,1)} %value_ref.1, f32[512,512]{1,0:T(8,128)} %filter_hbm.1), custom_call_target="tpu_custom_call" | custom-call | tf_op jit(solution)/shard_map/pack/pallas_call | solution.py:194
  1.9 0.0 copy-start.3
  2.0 0.0 copy-start.4
  2.0 0.0 copy-start.5
  2.0 0.0 copy-start.6
  2.0 0.0 copy-start.7
  2.0 0.0 copy-start.8
  2.0 62.9 %all_to_all.21 = f32[32,128,128]{2,1,0:T(8,128)S(1)} all-to-all(f32[32,128,128]{2,1,0:T(8,128)S(1)} %bitcast.11), channel_id=1, replica_groups=mesh['ctx'=32,'chan'=8] {'ctx'}, dimensions={0} | all-to-all | bytes 4194304 | tf_op jit(solution)/shard_map/all_to_all | solution.py:209
  64.9 0.0 copy-done.3
  64.9 0.0 copy-done.4
  64.9 0.0 copy-done.5
  65.0 0.0 copy-done.6
  65.0 0.0 copy-done.7
  65.0 5.1 %conv.1 = f32[2048,128]{1,0:T(8,128)S(1)} custom-call(f32[4096,128]{1,0:T(8,128)S(1)} %bitcast.10, bf16[512,256]{1,0:T(8,128)(2,1)S(1)} %copy-done.5, f32[128,128]{1,0:T(8,128)S(1)} %copy-done.8, f32[128,128]{1,0:T(8,128)S(1)} %copy-done.7, bf16[768,256]{1,0:T(8,128)(2,1)S(1)} %copy-done.4, bf16[768,256]{1,0:T(8,128)(2,1)S(1)} %copy-done.3, ...), custom_call_target="tpu_custom_call" | custom-call | tf_op jit(solution)/shard_map/conv/pallas_call | solution.py:212
  70.1 0.0 copy-start
  70.1 0.0 copy-start.1
  70.2 0.0 copy-start.2
  70.2 0.0 copy-start.10
  70.2 0.0 copy-start.9
  70.2 33.9 %all_to_all.22 = f32[32,64,128]{2,1,0:T(8,128)S(1)} all-to-all(f32[32,64,128]{2,1,0:T(8,128)S(1)} %bitcast.12), channel_id=1, replica_groups=mesh['ctx'=32,'chan'=8] {'ctx'}, dimensions={0} | all-to-all | bytes 2097152 | tf_op jit(solution)/shard_map/all_to_all | solution.py:219
  104.0 0.0 copy-done.1
  104.1 0.6 gate.1
  104.7 11.0 %all_to_all.23 = f32[8,1,512]{2,1,0:T(1,128)S(1)} all-to-all(f32[8,1,512]{2,1,0:T(1,128)S(1)} %copy.13), channel_id=1, replica_groups=mesh['ctx'=32,'chan'=8] {'chan'}, dimensions={0} | all-to-all | bytes 32768 | tf_op jit(solution)/shard_map/all_to_all | solution.py:230
  115.7 1.0 norm.1
  (7 shorter events, 0.0 us)
Async XLA Ops:
  1.9 63.0 %copy-start.3 = (bf16[768,256]{1,0:T(8,128)(2,1)S(1)}, bf16[768,256]{1,0:T(8,128)(2,1)}, u32[]{:S(2)}) copy-start(bf16[768,256]{1,0:T(8,128)(2,1)} %constant.16.clone.back_ref) | copy-start | bytes 1179652
  2.0 63.0 %copy-start.4 = (bf16[768,256]{1,0:T(8,128)(2,1)S(1)}, bf16[768,256]{1,0:T(8,128)(2,1)}, u32[]{:S(2)}) copy-start(bf16[768,256]{1,0:T(8,128)(2,1)} %constant.15.clone.fwd_ref) | copy-start | bytes 1179652
  2.0 63.0 %copy-start.5 = (bf16[512,256]{1,0:T(8,128)(2,1)S(1)}, bf16[512,256]{1,0:T(8,128)(2,1)}, u32[]{:S(2)}) copy-start(bf16[512,256]{1,0:T(8,128)(2,1)} %constant.12.clone.first_ref) | copy-start | bytes 786436
  2.0 63.0 %copy-start.6 = (bf16[256,256]{1,0:T(8,128)(2,1)S(1)}, bf16[256,256]{1,0:T(8,128)(2,1)}, u32[]{:S(2)}) copy-start(bf16[256,256]{1,0:T(8,128)(2,1)} %constant.17.clone.last_ref) | copy-start | bytes 393220
  2.0 63.0 %copy-start.7 = (f32[128,128]{1,0:T(8,128)S(1)}, f32[128,128]{1,0:T(8,128)}, u32[]{:S(2)}) copy-start(f32[128,128]{1,0:T(8,128)} %constant.14.clone.turn_im_ref) | copy-start | bytes 196612
  2.0 63.0 %copy-start.8 = (f32[128,128]{1,0:T(8,128)S(1)}, f32[128,128]{1,0:T(8,128)}, u32[]{:S(2)}) copy-start(f32[128,128]{1,0:T(8,128)} %constant.13.clone.turn_re_ref) | copy-start | bytes 196612
  70.1 33.9 %copy-start = (bf16[512,512]{1,0:T(8,128)(2,1)S(1)}, bf16[512,512]{1,0:T(8,128)(2,1)}, u32[]{:S(2)}) copy-start(bf16[512,512]{1,0:T(8,128)(2,1)} %key_ref.1) | copy-start | bytes 1572868
  70.1 33.9 %copy-start.1 = (bf16[512,512]{1,0:T(8,128)(2,1)S(1)}, bf16[512,512]{1,0:T(8,128)(2,1)}, u32[]{:S(2)}) copy-start(bf16[512,512]{1,0:T(8,128)(2,1)} %value_ref.1) | copy-start | bytes 1572868
  70.2 33.9 %copy-start.2 = (bf16[512,512]{1,0:T(8,128)(2,1)S(1)}, bf16[512,512]{1,0:T(8,128)(2,1)}, u32[]{:S(2)}) copy-start(bf16[512,512]{1,0:T(8,128)(2,1)} %query_ref.1) | copy-start | bytes 1572868
  70.2 33.9 %copy-start.10 = (f32[512]{0:T(512)S(1)}, f32[512]{0:T(512)}, u32[]{:S(2)}) copy-start(f32[512]{0:T(512)} %param.16) | copy-start | bytes 6148
  70.2 45.6 %copy-start.9 = (f32[512]{0:T(512)S(1)}, f32[512]{0:T(512)}, u32[]{:S(2)}) copy-start(f32[512]{0:T(512)} %param.17) | copy-start | bytes 6148

commit v5 on v4

--- a/solution.py
+++ b/solution.py
@@ -28,8 +28,12 @@
     m = np.arange(rows, dtype=np.float64)
     b = np.arange(cols, dtype=np.float64)
     first = 2.0 * math.pi * np.outer(m + 0.25, m) / rows
-    first_high, first_low = split_const(np.concatenate([np.cos(first), -np.sin(first)], axis=0))
-    first_table = np.block([[first_high, first_high], [first_low, np.zeros_like(first_low)]])
+    first_parts = []
+    for parity in range(2):
+        angle = first[: rows // 2, parity::2]
+        high, low = split_const(np.concatenate([np.cos(angle), -np.sin(angle)], axis=0))
+        first_parts.append(np.concatenate([high, high, low], axis=1))
+    first_table = np.concatenate(first_parts, axis=0)
     turn = 2.0 * math.pi * np.outer(m + 0.25, b) / length
     turn_re = np.cos(turn).astype(np.float32)
     turn_im = (-np.sin(turn)).astype(np.float32)
@@ -85,6 +89,7 @@
     group, share, data_ref, first_ref, turn_re_ref, turn_im_ref, fwd_ref, back_ref, last_ref, out_ref
 ):
     rows = turn_re_ref.shape[0]
+    half = rows // 2
     turn_re = jnp.concatenate([turn_re_ref[...]] * 2, axis=1)
     turn_im = jnp.concatenate([turn_im_ref[...]] * 2, axis=1)
 
@@ -92,15 +97,20 @@
         high, low = split(values)
         return dot(jnp.concatenate([high, low, high], axis=1), table_ref[...])
 
+    def half_sum(start, parity):
+        signal = data_ref[pl.ds(2 * share * parity + start, half, stride=4 * share), :]
+        kernel = data_ref[pl.ds(2 * share * parity + share + start, half, stride=4 * share), :]
+        high, low = split(jnp.concatenate([signal, kernel], axis=1))
+        table = first_ref[rows * parity : rows * (parity + 1)]
+        return dot(table, jnp.concatenate([high, low, high], axis=0))
+
     def first_stage(start):
         parts = []
         for c in range(start, start + group):
-            signal = data_ref[pl.ds(c, rows, stride=2 * share), :]
-            kernel = data_ref[pl.ds(share + c, rows, stride=2 * share), :]
-            high, low = split(jnp.concatenate([signal, kernel], axis=1))
-            spec = dot(first_ref[...], jnp.concatenate([high, low], axis=0))
-            re = spec[:rows] + spec[2 * rows : 3 * rows]
-            im = spec[rows : 2 * rows] + spec[3 * rows :]
+            even, odd = half_sum(c, 0), half_sum(c, 1)
+            total, difference = even + odd, even - odd
+            re = jnp.concatenate([total[:half], difference[:half]], axis=0)
+            im = jnp.concatenate([total[half:], difference[half:]], axis=0)
             out_re = re * turn_re - im * turn_im
             out_im = re * turn_im + im * turn_re
             parts.append(jnp.concatenate([out_re[:, :LANES], out_im[:, :LANES]], axis=1))
@@ -138,14 +148,14 @@
     groups = share // group
     turned, spectra, back = {}, {}, {}
     for step in range(groups + 3):
+        if step < groups:
+            turned[step] = first_stage(step * group)
         if 0 <= step - 1 < groups:
             spectra[step - 1] = product_of_spectra(turned.pop(step - 1))
-        if step < groups:
-            turned[step] = first_stage(step * group)
+        if 0 <= step - 2 < groups:
+            back[step - 2] = over_lanes(spectra.pop(step - 2), back_ref)
         if 0 <= step - 3 < groups:
             last_stage(back.pop(step - 3), (step - 3) * group)
-        if 0 <= step - 2 < groups:
-            back[step - 2] = over_lanes(spectra.pop(step - 2), back_ref)
 
 
 def gate_kernel(conv_ref, query_ref, key_ref, value_ref, skip_ref, gated_ref, square_ref):
@@ -163,15 +173,25 @@
         square_ref[:, at] = jnp.broadcast_to(total, (square_ref.shape[0], LANES))
 
 
-def norm_kernel(gated_ref, square_ref, gain_ref, out_ref):
+def norm_kernel(gated_ref, square_ref, gain_ref, out_hbm, out_ref, sems):
     total = jnp.sum(square_ref[...], axis=0, keepdims=True)
     inverse = lax.rsqrt(total / CH + 1e-05)
+    half = out_ref.shape[0] // 2
+    sends = []
     for top in range(0, out_ref.shape[0], LANES):
         down = slice(top, top + LANES)
         spread = jnp.broadcast_to(inverse[:, down], (LANES, LANES)).T
         for start in range(0, out_ref.shape[1], LANES):
             at = slice(start, start + LANES)
             out_ref[down, at] = (gated_ref[down, at] * spread * gain_ref[:, at]).astype(BF16)
+        if (top + LANES) % half == 0:
+            part = pl.ds(top + LANES - half, half)
+            sends.append(
+                pltpu.make_async_copy(out_ref.at[part], out_hbm.at[part], sems.at[len(sends)])
+            )
+            sends[-1].start()
+    for copy in sends:
+        copy.wait()
 
 
 def on_device(query_gate, key_branch, value_branch, conv_filter, skip_weight, norm_gain):
@@ -184,7 +204,6 @@
     params = pltpu.CompilerParams(vmem_limit_bytes=VMEM_BYTES)
     strip = pl.BlockSpec((LANES, channels), lambda a: (a, 0))
     row = pl.BlockSpec((1, channels), lambda a: (0, 0))
-    whole = (tokens, channels)
     whole = (tokens, channels)
     packed_shape = (blocks, pieces, 2, share, LANES)
     inputs = [
@@ -210,7 +229,7 @@
     gathered = gathered.reshape(rows * 2 * share, LANES)
     tables = transform_tables(rows, LANES)
     conv = pl.pallas_call(
-        functools.partial(conv_kernel, 4, share),
+        functools.partial(conv_kernel, 2, share),
         out_shape=jax.ShapeDtypeStruct((rows * share, LANES), F32),
         compiler_params=params,
         name="conv",
@@ -230,7 +249,10 @@
     square = lax.all_to_all(square, "chan", split_axis=0, concat_axis=0, tiled=True)
     return pl.pallas_call(
         norm_kernel,
-        out_shape=jax.ShapeDtypeStruct((tokens, channels), BF16),
+        in_specs=[pl.BlockSpec(memory_space=pltpu.VMEM)] * 3,
+        out_specs=pl.BlockSpec(memory_space=pltpu.HBM),
+        out_shape=jax.ShapeDtypeStruct(whole, BF16),
+        scratch_shapes=[pltpu.VMEM(whole, BF16), pltpu.SemaphoreType.DMA((2,))],
         compiler_params=params,
         name="norm",
     )(gated, square, norm_gain[None])

time: 117 us -> 117 us (level)
  no operation moved by 1% of the time
where the time goes in v5:
time: 117 us; the launch traced here: 116 us
  blocking collectives  108 us (92%)
  Pallas kernels  8.45 us (7%)
    all_to_all x1, blocking collectives, on_device(): lax.all_to_all(packed, 'ctx', split_axis=0, concat_axis=0, tiled=True)  62.9 us
    all_to_all x1, blocking collectives, on_device(): conv = lax.all_to_all(conv, 'ctx', split_axis=0, concat_axis=0, tiled=True)  33.9 us
    all_to_all x1, blocking collectives, on_device(): lax.all_to_all(square, 'chan', split_axis=0, concat_axis=0, tiled=True)  11 us
    pallas_call x1, Pallas kernels, on_device(): pl.pallas_call(functools.partial(conv_kernel, 2, share), out_shape=jax.Sh...  4.94 us

profile of v5, /device:TPU:16, one launch (start us, length us, event | category | flops | bytes accessed | tf_op | source)
XLA Modules:
  0.0 116.5 jit_solution(5609041969474988331)
XLA Ops:
  0.0 1.9 %pack.1 = f32[32,4,2,16,128]{4,3,2,1,0:T(8,128)S(1)} custom-call(bf16[512,512]{1,0:T(8,128)(2,1)} %key_ref.1, bf16[512,512]{1,0:T(8,128)(2,1)} %value_ref.1, f32[512,512]{1,0:T(8,128)} %filter_hbm.1), custom_call_target="tpu_custom_call" | custom-call | tf_op jit(solution)/shard_map/pack/pallas_call | solution.py:213
  1.9 0.0 copy-start.3
  2.0 0.0 copy-start.4
  2.0 0.0 copy-start.5
  2.0 0.0 copy-start.6
  2.0 0.0 copy-start.7
  2.0 0.0 copy-start.8
  2.0 62.9 %all_to_all.21 = f32[32,128,128]{2,1,0:T(8,128)S(1)} all-to-all(f32[32,128,128]{2,1,0:T(8,128)S(1)} %bitcast.11), channel_id=1, replica_groups=mesh['ctx'=32,'chan'=8] {'ctx'}, dimensions={0} | all-to-all | bytes 4194304 | tf_op jit(solution)/shard_map/all_to_all | solution.py:228
  64.9 0.0 copy-done.3
  64.9 0.0 copy-done.5
  65.0 0.0 copy-done.6
  65.0 0.0 copy-done.7
  65.0 0.0 copy-done.8
  65.0 4.9 %conv.1 = f32[2048,128]{1,0:T(8,128)S(1)} custom-call(f32[4096,128]{1,0:T(8,128)S(1)} %bitcast.10, bf16[256,192]{1,0:T(8,128)(2,1)S(1)} %copy-done.6, f32[128,128]{1,0:T(8,128)S(1)} %copy-done.8, f32[128,128]{1,0:T(8,128)S(1)} %copy-done.7, bf16[768,256]{1,0:T(8,128)(2,1)S(1)} %copy-done.4, bf16[768,256]{1,0:T(8,128)(2,1)S(1)} %copy-done.3, ...), custom_call_target="tpu_custom_call" | custom-call | tf_op jit(solution)/shard_map/conv/pallas_call | solution.py:231
  69.9 0.0 copy-start
  69.9 0.0 copy-start.1
  70.0 0.0 copy-start.2
  70.0 0.0 copy-start.10
  70.0 0.0 copy-start.9
  70.0 33.9 %all_to_all.22 = f32[32,64,128]{2,1,0:T(8,128)S(1)} all-to-all(f32[32,64,128]{2,1,0:T(8,128)S(1)} %bitcast.13), channel_id=1, replica_groups=mesh['ctx'=32,'chan'=8] {'ctx'}, dimensions={0} | all-to-all | bytes 2097152 | tf_op jit(solution)/shard_map/all_to_all | solution.py:238
  103.8 0.0 copy-done.1
  103.9 0.6 gate.1
  104.5 11.0 %all_to_all.23 = f32[8,1,512]{2,1,0:T(1,128)S(1)} all-to-all(f32[8,1,512]{2,1,0:T(1,128)S(1)} %copy.13), channel_id=1, replica_groups=mesh['ctx'=32,'chan'=8] {'chan'}, dimensions={0} | all-to-all | bytes 32768 | tf_op jit(solution)/shard_map/all_to_all | solution.py:249
  115.5 1.0 norm.1
  (7 shorter events, 0.0 us)
Async XLA Ops:
  1.9 63.0 %copy-start.3 = (bf16[768,256]{1,0:T(8,128)(2,1)S(1)}, bf16[768,256]{1,0:T(8,128)(2,1)}, u32[]{:S(2)}) copy-start(bf16[768,256]{1,0:T(8,128)(2,1)} %constant.16.clone.back_ref) | copy-start | bytes 1179652
  2.0 63.0 %copy-start.4 = (bf16[768,256]{1,0:T(8,128)(2,1)S(1)}, bf16[768,256]{1,0:T(8,128)(2,1)}, u32[]{:S(2)}) copy-start(bf16[768,256]{1,0:T(8,128)(2,1)} %constant.15.clone.fwd_ref) | copy-start | bytes 1179652
  2.0 63.0 %copy-start.5 = (bf16[256,256]{1,0:T(8,128)(2,1)S(1)}, bf16[256,256]{1,0:T(8,128)(2,1)}, u32[]{:S(2)}) copy-start(bf16[256,256]{1,0:T(8,128)(2,1)} %constant.17.clone.last_ref) | copy-start | bytes 393220
  2.0 63.0 %copy-start.6 = (bf16[256,192]{1,0:T(8,128)(2,1)S(1)}, bf16[256,192]{1,0:T(8,128)(2,1)}, u32[]{:S(2)}) copy-start(bf16[256,192]{1,0:T(8,128)(2,1)} %constant.12.clone.first_ref) | copy-start | bytes 294916
  2.0 63.0 %copy-start.7 = (f32[128,128]{1,0:T(8,128)S(1)}, f32[128,128]{1,0:T(8,128)}, u32[]{:S(2)}) copy-start(f32[128,128]{1,0:T(8,128)} %constant.14.clone.turn_im_ref) | copy-start | bytes 196612
  2.0 63.0 %copy-start.8 = (f32[128,128]{1,0:T(8,128)S(1)}, f32[128,128]{1,0:T(8,128)}, u32[]{:S(2)}) copy-start(f32[128,128]{1,0:T(8,128)} %constant.13.clone.turn_re_ref) | copy-start | bytes 196612
  69.9 33.9 %copy-start = (bf16[512,512]{1,0:T(8,128)(2,1)S(1)}, bf16[512,512]{1,0:T(8,128)(2,1)}, u32[]{:S(2)}) copy-start(bf16[512,512]{1,0:T(8,128)(2,1)} %key_ref.1) | copy-start | bytes 1572868
  69.9 33.9 %copy-start.1 = (bf16[512,512]{1,0:T(8,128)(2,1)S(1)}, bf16[512,512]{1,0:T(8,128)(2,1)}, u32[]{:S(2)}) copy-start(bf16[512,512]{1,0:T(8,128)(2,1)} %value_ref.1) | copy-start | bytes 1572868
  70.0 33.9 %copy-start.2 = (bf16[512,512]{1,0:T(8,128)(2,1)S(1)}, bf16[512,512]{1,0:T(8,128)(2,1)}, u32[]{:S(2)}) copy-start(bf16[512,512]{1,0:T(8,128)(2,1)} %query_ref.1) | copy-start | bytes 1572868
  70.0 33.9 %copy-start.10 = (f32[512]{0:T(512)S(1)}, f32[512]{0:T(512)}, u32[]{:S(2)}) copy-start(f32[512]{0:T(512)} %param.16) | copy-start | bytes 6148
  70.0 45.6 %copy-start.9 = (f32[512]{0:T(512)S(1)}, f32[512]{0:T(512)}, u32[]{:S(2)}) copy-start(f32[512]{0:T(512)} %param.17) | copy-start | bytes 6148

commit v6 on v5

--- a/solution.py
+++ b/solution.py
@@ -158,13 +158,15 @@
             last_stage(back.pop(step - 3), (step - 3) * group)
 
 
-def gate_kernel(conv_ref, query_ref, key_ref, value_ref, skip_ref, gated_ref, square_ref):
+def gate_kernel(
+    conv_ref, query_ref, key_ref, value_ref, skip_ref, gain_ref, gated_ref, square_ref
+):
     for piece in range(conv_ref.shape[1]):
         at = slice(piece * LANES, (piece + 1) * LANES)
         conv = conv_ref[:, piece].reshape(-1, LANES).T
         product = key_ref[at, :].astype(F32) * value_ref[at, :].astype(F32)
         gated = query_ref[at, :].astype(F32) * (conv + skip_ref[...] * product)
-        gated_ref[at, :] = gated
+        gated_ref[at, :] = gated * gain_ref[...]
         square = gated * gated
         folded = square[:, :LANES]
         for start in range(LANES, square.shape[1], LANES):
@@ -173,19 +175,19 @@
         square_ref[:, at] = jnp.broadcast_to(total, (square_ref.shape[0], LANES))
 
 
-def norm_kernel(gated_ref, square_ref, gain_ref, out_hbm, out_ref, sems):
+def norm_kernel(gated_ref, square_ref, out_hbm, out_ref, sems):
     total = jnp.sum(square_ref[...], axis=0, keepdims=True)
     inverse = lax.rsqrt(total / CH + 1e-05)
-    half = out_ref.shape[0] // 2
+    part_rows = out_ref.shape[0] // 4
     sends = []
     for top in range(0, out_ref.shape[0], LANES):
         down = slice(top, top + LANES)
         spread = jnp.broadcast_to(inverse[:, down], (LANES, LANES)).T
         for start in range(0, out_ref.shape[1], LANES):
             at = slice(start, start + LANES)
-            out_ref[down, at] = (gated_ref[down, at] * spread * gain_ref[:, at]).astype(BF16)
-        if (top + LANES) % half == 0:
-            part = pl.ds(top + LANES - half, half)
+            out_ref[down, at] = (gated_ref[down, at] * spread).astype(BF16)
+        if (top + LANES) % part_rows == 0:
+            part = pl.ds(top + LANES - part_rows, part_rows)
             sends.append(
                 pltpu.make_async_copy(out_ref.at[part], out_hbm.at[part], sems.at[len(sends)])
             )
@@ -245,17 +247,17 @@
         ],
         compiler_params=params,
         name="gate",
-    )(conv, query_gate, key_branch, value_branch, skip_weight[None])
+    )(conv, query_gate, key_branch, value_branch, skip_weight[None], norm_gain[None])
     square = lax.all_to_all(square, "chan", split_axis=0, concat_axis=0, tiled=True)
     return pl.pallas_call(
         norm_kernel,
-        in_specs=[pl.BlockSpec(memory_space=pltpu.VMEM)] * 3,
+        in_specs=[pl.BlockSpec(memory_space=pltpu.VMEM)] * 2,
         out_specs=pl.BlockSpec(memory_space=pltpu.HBM),
         out_shape=jax.ShapeDtypeStruct(whole, BF16),
-        scratch_shapes=[pltpu.VMEM(whole, BF16), pltpu.SemaphoreType.DMA((2,))],
+        scratch_shapes=[pltpu.VMEM(whole, BF16), pltpu.SemaphoreType.DMA((4,))],
         compiler_params=params,
         name="norm",
-    )(gated, square, norm_gain[None])
+    )(gated, square)
 
 
 def solution(mesh):

time: 117 us -> 117 us (level)
  no operation moved by 1% of the time
where the time goes in v6:
time: 117 us; the launch traced here: 116 us
  blocking collectives  108 us (92%)
  Pallas kernels  8.44 us (7%)
    all_to_all x1, blocking collectives, on_device(): lax.all_to_all(packed, 'ctx', split_axis=0, concat_axis=0, tiled=True)  62.9 us
    all_to_all x1, blocking collectives, on_device(): conv = lax.all_to_all(conv, 'ctx', split_axis=0, concat_axis=0, tiled=True)  33.9 us
    all_to_all x1, blocking collectives, on_device(): lax.all_to_all(square, 'chan', split_axis=0, concat_axis=0, tiled=True)  11 us
    pallas_call x1, Pallas kernels, on_device(): pl.pallas_call(functools.partial(conv_kernel, 2, share), out_shape=jax.Sh...  4.94 us

profile of v6, /device:TPU:16, one launch (start us, length us, event | category | flops | bytes accessed | tf_op | source)
XLA Modules:
  0.0 116.5 jit_solution(7571496214312107283)
XLA Ops:
  0.0 1.9 %pack.1 = f32[32,4,2,16,128]{4,3,2,1,0:T(8,128)S(1)} custom-call(bf16[512,512]{1,0:T(8,128)(2,1)} %key_ref.1, bf16[512,512]{1,0:T(8,128)(2,1)} %value_ref.1, f32[512,512]{1,0:T(8,128)} %filter_hbm.1), custom_call_target="tpu_custom_call" | custom-call | tf_op jit(solution)/shard_map/pack/pallas_call | solution.py:215
  1.9 0.0 copy-start.3
  2.0 0.0 copy-start.4
  2.0 0.0 copy-start.5
  2.0 0.0 copy-start.6
  2.0 0.0 copy-start.7
  2.0 0.0 copy-start.8
  2.0 62.9 %all_to_all.21 = f32[32,128,128]{2,1,0:T(8,128)S(1)} all-to-all(f32[32,128,128]{2,1,0:T(8,128)S(1)} %bitcast.11), channel_id=1, replica_groups=mesh['ctx'=32,'chan'=8] {'ctx'}, dimensions={0} | all-to-all | bytes 4194304 | tf_op jit(solution)/shard_map/all_to_all | solution.py:230
  64.9 0.0 copy-done.3
  64.9 0.0 copy-done.5
  65.0 0.0 copy-done.6
  65.0 0.0 copy-done.7
  65.0 0.0 copy-done.8
  65.0 4.9 %conv.1 = f32[2048,128]{1,0:T(8,128)S(1)} custom-call(f32[4096,128]{1,0:T(8,128)S(1)} %bitcast.10, bf16[256,192]{1,0:T(8,128)(2,1)S(1)} %copy-done.6, f32[128,128]{1,0:T(8,128)S(1)} %copy-done.8, f32[128,128]{1,0:T(8,128)S(1)} %copy-done.7, bf16[768,256]{1,0:T(8,128)(2,1)S(1)} %copy-done.4, bf16[768,256]{1,0:T(8,128)(2,1)S(1)} %copy-done.3, ...), custom_call_target="tpu_custom_call" | custom-call | tf_op jit(solution)/shard_map/conv/pallas_call | solution.py:233
  69.9 0.0 copy-start
  69.9 0.0 copy-start.1
  70.0 0.0 copy-start.2
  70.0 0.0 copy-start.9
  70.0 0.0 copy-start.10
  70.0 33.9 %all_to_all.22 = f32[32,64,128]{2,1,0:T(8,128)S(1)} all-to-all(f32[32,64,128]{2,1,0:T(8,128)S(1)} %bitcast.13), channel_id=1, replica_groups=mesh['ctx'=32,'chan'=8] {'ctx'}, dimensions={0} | all-to-all | bytes 2097152 | tf_op jit(solution)/shard_map/all_to_all | solution.py:240
  103.8 0.0 copy-done.1
  103.9 0.6 gate.1
  104.5 11.0 %all_to_all.23 = f32[8,1,512]{2,1,0:T(1,128)S(1)} all-to-all(f32[8,1,512]{2,1,0:T(1,128)S(1)} %copy.13), channel_id=1, replica_groups=mesh['ctx'=32,'chan'=8] {'chan'}, dimensions={0} | all-to-all | bytes 32768 | tf_op jit(solution)/shard_map/all_to_all | solution.py:251
  115.6 0.9 norm.1
  (7 shorter events, 0.0 us)
Async XLA Ops:
  1.9 63.0 %copy-start.3 = (bf16[768,256]{1,0:T(8,128)(2,1)S(1)}, bf16[768,256]{1,0:T(8,128)(2,1)}, u32[]{:S(2)}) copy-start(bf16[768,256]{1,0:T(8,128)(2,1)} %constant.16.clone.back_ref) | copy-start | bytes 1179652
  2.0 63.0 %copy-start.4 = (bf16[768,256]{1,0:T(8,128)(2,1)S(1)}, bf16[768,256]{1,0:T(8,128)(2,1)}, u32[]{:S(2)}) copy-start(bf16[768,256]{1,0:T(8,128)(2,1)} %constant.15.clone.fwd_ref) | copy-start | bytes 1179652
  2.0 63.0 %copy-start.5 = (bf16[256,256]{1,0:T(8,128)(2,1)S(1)}, bf16[256,256]{1,0:T(8,128)(2,1)}, u32[]{:S(2)}) copy-start(bf16[256,256]{1,0:T(8,128)(2,1)} %constant.17.clone.last_ref) | copy-start | bytes 393220
  2.0 63.0 %copy-start.6 = (bf16[256,192]{1,0:T(8,128)(2,1)S(1)}, bf16[256,192]{1,0:T(8,128)(2,1)}, u32[]{:S(2)}) copy-start(bf16[256,192]{1,0:T(8,128)(2,1)} %constant.12.clone.first_ref) | copy-start | bytes 294916
  2.0 63.0 %copy-start.7 = (f32[128,128]{1,0:T(8,128)S(1)}, f32[128,128]{1,0:T(8,128)}, u32[]{:S(2)}) copy-start(f32[128,128]{1,0:T(8,128)} %constant.14.clone.turn_im_ref) | copy-start | bytes 196612
  2.0 63.0 %copy-start.8 = (f32[128,128]{1,0:T(8,128)S(1)}, f32[128,128]{1,0:T(8,128)}, u32[]{:S(2)}) copy-start(f32[128,128]{1,0:T(8,128)} %constant.13.clone.turn_re_ref) | copy-start | bytes 196612
  69.9 33.9 %copy-start = (bf16[512,512]{1,0:T(8,128)(2,1)S(1)}, bf16[512,512]{1,0:T(8,128)(2,1)}, u32[]{:S(2)}) copy-start(bf16[512,512]{1,0:T(8,128)(2,1)} %key_ref.1) | copy-start | bytes 1572868
  69.9 33.9 %copy-start.1 = (bf16[512,512]{1,0:T(8,128)(2,1)S(1)}, bf16[512,512]{1,0:T(8,128)(2,1)}, u32[]{:S(2)}) copy-start(bf16[512,512]{1,0:T(8,128)(2,1)} %value_ref.1) | copy-start | bytes 1572868
  70.0 33.9 %copy-start.2 = (bf16[512,512]{1,0:T(8,128)(2,1)S(1)}, bf16[512,512]{1,0:T(8,128)(2,1)}, u32[]{:S(2)}) copy-start(bf16[512,512]{1,0:T(8,128)(2,1)} %query_ref.1) | copy-start | bytes 1572868
  70.0 33.9 %copy-start.9 = (f32[512]{0:T(512)S(1)}, f32[512]{0:T(512)}, u32[]{:S(2)}) copy-start(f32[512]{0:T(512)} %param.16) | copy-start | bytes 6148
  70.0 33.9 %copy-start.10 = (f32[512]{0:T(512)S(1)}, f32[512]{0:T(512)}, u32[]{:S(2)}) copy-start(f32[512]{0:T(512)} %param.17) | copy-start | bytes 6148

commit v7 on v5

--- a/solution.py
+++ b/solution.py
@@ -159,18 +159,21 @@
 
 
 def gate_kernel(conv_ref, query_ref, key_ref, value_ref, skip_ref, gated_ref, square_ref):
+    per_tile = LANES // conv_ref.shape[2]
     for piece in range(conv_ref.shape[1]):
-        at = slice(piece * LANES, (piece + 1) * LANES)
-        conv = conv_ref[:, piece].reshape(-1, LANES).T
-        product = key_ref[at, :].astype(F32) * value_ref[at, :].astype(F32)
-        gated = query_ref[at, :].astype(F32) * (conv + skip_ref[...] * product)
-        gated_ref[at, :] = gated
-        square = gated * gated
-        folded = square[:, :LANES]
-        for start in range(LANES, square.shape[1], LANES):
-            folded = folded + square[:, start : start + LANES]
+        down = slice(piece * LANES, (piece + 1) * LANES)
+        folded = None
+        for tile in range(gated_ref.shape[1] // LANES):
+            at = slice(tile * LANES, (tile + 1) * LANES)
+            owners = slice(tile * per_tile, (tile + 1) * per_tile)
+            conv = conv_ref[owners, piece].reshape(LANES, LANES).T
+            product = key_ref[down, at].astype(F32) * value_ref[down, at].astype(F32)
+            gated = query_ref[down, at].astype(F32) * (conv + skip_ref[:, at] * product)
+            gated_ref[down, at] = gated
+            square = gated * gated
+            folded = square if folded is None else folded + square
         total = jnp.sum(folded.T, axis=0, keepdims=True)
-        square_ref[:, at] = jnp.broadcast_to(total, (square_ref.shape[0], LANES))
+        square_ref[:, down] = jnp.broadcast_to(total, (square_ref.shape[0], LANES))
 
 
 def norm_kernel(gated_ref, square_ref, gain_ref, out_hbm, out_ref, sems):

time: 117 us -> 117 us (level)
  no operation moved by 1% of the time
where the time goes in v7:
time: 117 us; the launch traced here: 116 us
  blocking collectives  108 us (92%)
  Pallas kernels  8.45 us (7%)
    all_to_all x1, blocking collectives, on_device(): lax.all_to_all(packed, 'ctx', split_axis=0, concat_axis=0, tiled=True)  62.9 us
    all_to_all x1, blocking collectives, on_device(): conv = lax.all_to_all(conv, 'ctx', split_axis=0, concat_axis=0, tiled=True)  33.9 us
    all_to_all x1, blocking collectives, on_device(): lax.all_to_all(square, 'chan', split_axis=0, concat_axis=0, tiled=True)  11 us
    pallas_call x1, Pallas kernels, on_device(): pl.pallas_call(functools.partial(conv_kernel, 2, share), out_shape=jax.Sh...  4.94 us

profile of v7, /device:TPU:16, one launch (start us, length us, event | category | flops | bytes accessed | tf_op | source)
XLA Modules:
  0.0 116.5 jit_solution(4688334896868587019)
XLA Ops:
  0.0 1.9 %pack.1 = f32[32,4,2,16,128]{4,3,2,1,0:T(8,128)S(1)} custom-call(bf16[512,512]{1,0:T(8,128)(2,1)} %key_ref.1, bf16[512,512]{1,0:T(8,128)(2,1)} %value_ref.1, f32[512,512]{1,0:T(8,128)} %filter_hbm.1), custom_call_target="tpu_custom_call" | custom-call | tf_op jit(solution)/shard_map/pack/pallas_call | solution.py:216
  1.9 0.0 copy-start.3
  2.0 0.0 copy-start.4
  2.0 0.0 copy-start.5
  2.0 0.0 copy-start.6
  2.0 0.0 copy-start.7
  2.0 0.0 copy-start.8
  2.0 62.9 %all_to_all.21 = f32[32,128,128]{2,1,0:T(8,128)S(1)} all-to-all(f32[32,128,128]{2,1,0:T(8,128)S(1)} %bitcast.11), channel_id=1, replica_groups=mesh['ctx'=32,'chan'=8] {'ctx'}, dimensions={0} | all-to-all | bytes 4194304 | tf_op jit(solution)/shard_map/all_to_all | solution.py:231
  64.9 0.0 copy-done.3
  64.9 0.0 copy-done.5
  65.0 0.0 copy-done.6
  65.0 0.0 copy-done.7
  65.0 0.0 copy-done.8
  65.0 4.9 %conv.1 = f32[2048,128]{1,0:T(8,128)S(1)} custom-call(f32[4096,128]{1,0:T(8,128)S(1)} %bitcast.10, bf16[256,192]{1,0:T(8,128)(2,1)S(1)} %copy-done.6, f32[128,128]{1,0:T(8,128)S(1)} %copy-done.8, f32[128,128]{1,0:T(8,128)S(1)} %copy-done.7, bf16[768,256]{1,0:T(8,128)(2,1)S(1)} %copy-done.4, bf16[768,256]{1,0:T(8,128)(2,1)S(1)} %copy-done.3, ...), custom_call_target="tpu_custom_call" | custom-call | tf_op jit(solution)/shard_map/conv/pallas_call | solution.py:234
  69.9 0.0 copy-start
  69.9 0.0 copy-start.1
  70.0 0.0 copy-start.2
  70.0 0.0 copy-start.10
  70.0 0.0 copy-start.9
  70.0 33.9 %all_to_all.22 = f32[32,64,128]{2,1,0:T(8,128)S(1)} all-to-all(f32[32,64,128]{2,1,0:T(8,128)S(1)} %bitcast.13), channel_id=1, replica_groups=mesh['ctx'=32,'chan'=8] {'ctx'}, dimensions={0} | all-to-all | bytes 2097152 | tf_op jit(solution)/shard_map/all_to_all | solution.py:241
  103.8 0.0 copy-done.1
  103.9 0.6 gate.1
  104.5 11.0 %all_to_all.23 = f32[8,1,512]{2,1,0:T(1,128)S(1)} all-to-all(f32[8,1,512]{2,1,0:T(1,128)S(1)} %copy.13), channel_id=1, replica_groups=mesh['ctx'=32,'chan'=8] {'chan'}, dimensions={0} | all-to-all | bytes 32768 | tf_op jit(solution)/shard_map/all_to_all | solution.py:252
  115.5 1.0 norm.1
  (7 shorter events, 0.0 us)
Async XLA Ops:
  1.9 63.0 %copy-start.3 = (bf16[768,256]{1,0:T(8,128)(2,1)S(1)}, bf16[768,256]{1,0:T(8,128)(2,1)}, u32[]{:S(2)}) copy-start(bf16[768,256]{1,0:T(8,128)(2,1)} %constant.16.clone.back_ref) | copy-start | bytes 1179652
  2.0 63.0 %copy-start.4 = (bf16[768,256]{1,0:T(8,128)(2,1)S(1)}, bf16[768,256]{1,0:T(8,128)(2,1)}, u32[]{:S(2)}) copy-start(bf16[768,256]{1,0:T(8,128)(2,1)} %constant.15.clone.fwd_ref) | copy-start | bytes 1179652
  2.0 63.0 %copy-start.5 = (bf16[256,256]{1,0:T(8,128)(2,1)S(1)}, bf16[256,256]{1,0:T(8,128)(2,1)}, u32[]{:S(2)}) copy-start(bf16[256,256]{1,0:T(8,128)(2,1)} %constant.17.clone.last_ref) | copy-start | bytes 393220
  2.0 63.0 %copy-start.6 = (bf16[256,192]{1,0:T(8,128)(2,1)S(1)}, bf16[256,192]{1,0:T(8,128)(2,1)}, u32[]{:S(2)}) copy-start(bf16[256,192]{1,0:T(8,128)(2,1)} %constant.12.clone.first_ref) | copy-start | bytes 294916
  2.0 63.0 %copy-start.7 = (f32[128,128]{1,0:T(8,128)S(1)}, f32[128,128]{1,0:T(8,128)}, u32[]{:S(2)}) copy-start(f32[128,128]{1,0:T(8,128)} %constant.14.clone.turn_im_ref) | copy-start | bytes 196612
  2.0 63.0 %copy-start.8 = (f32[128,128]{1,0:T(8,128)S(1)}, f32[128,128]{1,0:T(8,128)}, u32[]{:S(2)}) copy-start(f32[128,128]{1,0:T(8,128)} %constant.13.clone.turn_re_ref) | copy-start | bytes 196612
  69.9 33.9 %copy-start = (bf16[512,512]{1,0:T(8,128)(2,1)S(1)}, bf16[512,512]{1,0:T(8,128)(2,1)}, u32[]{:S(2)}) copy-start(bf16[512,512]{1,0:T(8,128)(2,1)} %key_ref.1) | copy-start | bytes 1572868
  69.9 33.9 %copy-start.1 = (bf16[512,512]{1,0:T(8,128)(2,1)S(1)}, bf16[512,512]{1,0:T(8,128)(2,1)}, u32[]{:S(2)}) copy-start(bf16[512,512]{1,0:T(8,128)(2,1)} %value_ref.1) | copy-start | bytes 1572868
  70.0 33.9 %copy-start.2 = (bf16[512,512]{1,0:T(8,128)(2,1)S(1)}, bf16[512,512]{1,0:T(8,128)(2,1)}, u32[]{:S(2)}) copy-start(bf16[512,512]{1,0:T(8,128)(2,1)} %query_ref.1) | copy-start | bytes 1572868
  70.0 33.9 %copy-start.10 = (f32[512]{0:T(512)S(1)}, f32[512]{0:T(512)}, u32[]{:S(2)}) copy-start(f32[512]{0:T(512)} %param.16) | copy-start | bytes 6148
  70.0 45.6 %copy-start.9 = (f32[512]{0:T(512)S(1)}, f32[512]{0:T(512)}, u32[]{:S(2)}) copy-start(f32[512]{0:T(512)} %param.17) | copy-start | bytes 6148
